TPU v7x, 256 devices: a whole 4x4x8 slice. The times are simulated.
256 devices in a mesh: row: 16 (over x, y_hi, core), col: 16 (over y_lo, z).
Axes of the slice: x: 4, y: 4 (y_hi: 2, y_lo: 2; y = y_hi * 2 + y_lo), z: 8, core: 2. Of those that a mesh axis runs over, the one named last changes fastest.
Arguments:
- pair_out: bfloat16 [512, 768, 128], P('row', 'col'), may hold values from -6 to 6
- pair_left: bfloat16 [512, 512, 128], P('col', 'row'), may hold values from -6 to 6
- pair_right: bfloat16 [512, 768, 128], P('row', 'col'), may hold values from -6 to 6
- ln_gain: float32 [128], replicated, may hold values from 0.1 to 1.9
- ln_bias: float32 [128], replicated, may hold values from -3 to 3
- w_left: bfloat16 [128, 256], replicated, may hold values from -0.5 to 0.5
- w_right: bfloat16 [128, 256], replicated, may hold values from -0.5 to 0.5
- w_gate: bfloat16 [128, 128], replicated, may hold values from -0.5 to 0.5
- w_out: bfloat16 [128, 128], replicated, may hold values from -0.5 to 0.5
- out_gain: float32 [128], replicated, may hold values from 0.1 to 1.9
- out_bias: float32 [128], replicated, may hold values from -3 to 3
- cotangent: bfloat16 [512, 768, 128], P('row', 'col'), may hold values from -6 to 6
Outputs:
- result: bfloat16 [512, 768, 128], P('row', 'col')
- grad_out: bfloat16 [512, 768, 128], P('row', 'col')
- grad_left: bfloat16 [512, 512, 128], P('col', 'row')
- grad_right: bfloat16 [512, 768, 128], P('row', 'col')
All inputs are finite; a program needn't handle non-finite values.
Results may differ from a plain program's by a relative error of at most 0.025.
Values may be sent and summed in bfloat16 or wider, within the bound.
A program may use at most 128 MiB of HBM per device.

v0:
```python
import jax
import jax.numpy as jnp
from jax import lax
from jax.sharding import PartitionSpec as P


def normalize(values, gain, bias):
    center = values - jnp.mean(values, axis=-1, keepdims=True)
    inverse = lax.rsqrt(jnp.mean(center * center, axis=-1, keepdims=True) + 1e-05)
    standard = center * inverse
    return (standard * gain + bias, standard, inverse)


def norm_back(upstream, standard, inverse, gain):
    scaled = upstream * gain
    return inverse * (
        scaled
        - jnp.mean(scaled, axis=-1, keepdims=True)
        - standard * jnp.mean(scaled * standard, axis=-1, keepdims=True)
    )


def project(pair_tile, gain, bias, weight):
    normed, standard, inverse = normalize(pair_tile.astype(jnp.float32), gain, bias)
    normed = normed.astype(jnp.bfloat16)
    hidden_width = weight.shape[1] // 2
    pre_act = jnp.dot(
        normed.reshape(-1, normed.shape[-1]), weight, preferred_element_type=jnp.float32
    )
    pre_act = pre_act.reshape(pair_tile.shape[:-1] + (2 * hidden_width,))
    gated = (jax.nn.sigmoid(pre_act[..., hidden_width:]) * pre_act[..., :hidden_width]).astype(
        jnp.bfloat16
    )
    return (gated, pre_act, standard, inverse)


def project_back(d_gated, pre_act, standard, inverse, gain, weight):
    hidden_width = weight.shape[1] // 2
    squash = jax.nn.sigmoid(pre_act[..., hidden_width:])
    values_half = pre_act[..., :hidden_width]
    d_pre = jnp.concatenate(
        [d_gated * squash, d_gated * values_half * squash * (1.0 - squash)], axis=-1
    )
    d_pre = d_pre.astype(jnp.bfloat16)
    d_normed = jnp.dot(
        d_pre.reshape(-1, 2 * hidden_width), weight.T, preferred_element_type=jnp.float32
    )
    return norm_back(d_normed.reshape(standard.shape), standard, inverse, gain).astype(jnp.bfloat16)


def per_device(
    pair_out,
    pair_left,
    pair_right,
    ln_gain,
    ln_bias,
    w_left,
    w_right,
    w_gate,
    w_out,
    out_gain,
    out_bias,
    cotangent,
):
    features = pair_out.shape[2]
    hidden_width = w_out.shape[0]
    left_gated, left_pre, left_std, left_inv = project(pair_left, ln_gain, ln_bias, w_left)
    right_gated, right_pre, right_std, right_inv = project(pair_right, ln_gain, ln_bias, w_right)
    left_full = lax.all_gather(left_gated, "col", axis=0, tiled=True)
    right_full = lax.all_gather(right_gated, "row", axis=0, tiled=True)
    triangle = jnp.einsum("kih,kjh->ijh", left_full, right_full, preferred_element_type=jnp.float32)
    tri_normed, tri_std, tri_inv = normalize(triangle, out_gain, out_bias)
    tri_normed = tri_normed.astype(jnp.bfloat16)
    out_normed, out_std, out_inv = normalize(pair_out.astype(jnp.float32), ln_gain, ln_bias)
    out_normed = out_normed.astype(jnp.bfloat16)
    out_gate = jax.nn.sigmoid(
        jnp.dot(out_normed.reshape(-1, features), w_gate, preferred_element_type=jnp.float32)
    )
    out_proj = jnp.dot(
        tri_normed.reshape(-1, hidden_width), w_out, preferred_element_type=jnp.float32
    )
    result = (out_gate * out_proj).astype(jnp.bfloat16).reshape(pair_out.shape)
    upstream = cotangent.reshape(-1, features).astype(jnp.float32)
    d_proj = (upstream * out_gate).astype(jnp.bfloat16)
    d_gate = (upstream * out_proj * out_gate * (1.0 - out_gate)).astype(jnp.bfloat16)
    d_outn = jnp.dot(d_gate, w_gate.T, preferred_element_type=jnp.float32).reshape(pair_out.shape)
    grad_out = norm_back(d_outn, out_std, out_inv, ln_gain).astype(jnp.bfloat16)
    d_trin = jnp.dot(d_proj, w_out.T, preferred_element_type=jnp.float32).reshape(triangle.shape)
    d_triangle = norm_back(d_trin, tri_std, tri_inv, out_gain).astype(jnp.bfloat16)
    d_left = lax.psum_scatter(
        jnp.einsum(
            "ijh,kjh->kih", d_triangle, right_full, preferred_element_type=jnp.float32
        ).astype(jnp.bfloat16),
        "col",
        scatter_dimension=0,
        tiled=True,
    ).astype(jnp.float32)
    d_right = lax.psum_scatter(
        jnp.einsum(
            "ijh,kih->kjh", d_triangle, left_full, preferred_element_type=jnp.float32
        ).astype(jnp.bfloat16),
        "row",
        scatter_dimension=0,
        tiled=True,
    ).astype(jnp.float32)
    grad_left = project_back(d_left, left_pre, left_std, left_inv, ln_gain, w_left)
    grad_right = project_back(d_right, right_pre, right_std, right_inv, ln_gain, w_right)
    return (result, grad_out, grad_left, grad_right)


def solution(mesh):
    return jax.shard_map(
        per_device,
        mesh=mesh,
        in_specs=(
            P("row", "col", None),
            P("col", "row", None),
            P("row", "col", None),
            P(),
            P(),
            P(),
            P(),
            P(),
            P(),
            P(),
            P(),
            P("row", "col", None),
        ),
        out_specs=(
            P("row", "col", None),
            P("row", "col", None),
            P("col", "row", None),
            P("row", "col", None),
        ),
        check_vma=False,
    )
```

profile of v0, /device:TPU:1, one launch (start us, length us, event | category | flops | bytes accessed | tf_op | source)
XLA Modules:
  0.0 410.4 jit_solution(10935491577532320342)
XLA Ops:
  7.2 1.2 convert_reduce_fusion.2
  8.5 1.3 fusion.53
  9.9 1.4 fusion.75
  14.7 1.1 copy-done.2
  20.2 2.8 copy.34
  23.0 62.2 %all-gather.5.cloned.1.call-done = bf16[512,32,128]{2,1,0:T(8,128)(2,1)} async-done(((bf16[32,32,128]{2,1,0:T(8,128)(2,1)}), bf16[512,32,128]{2,1,0:T(8,128)(2,1)}) %all-gather.5.cloned.1.call-update) | async-done | bytes 4194320 | tf_op jit(solution)/shard_map/all_gather | solution.py:69
  85.2 23.0 %copy.37 = bf16[512,32,128]{1,0,2:T(8,128)(2,1)} copy(bf16[512,32,128]{2,1,0:T(8,128)(2,1)} %all-gather.5.cloned.1.call-done) | data formatting | bytes 8388608 | tf_op jit(solution)/shard_map/all_gather | solution.py:69
  108.2 56.2 %all-gather.3.cloned.1.call-done = bf16[512,48,128]{2,1,0:T(8,128)(2,1)} async-done(((bf16[32,48,128]{2,1,0:T(8,128)(2,1)}), bf16[512,48,128]{2,1,0:T(8,128)(2,1)}) %all-gather.3.cloned.1.call-update) | async-done | bytes 6291472 | tf_op jit(solution)/shard_map/all_gather | solution.py:70
  164.4 23.1 %copy.31 = bf16[512,48,128]{1,0,2:T(8,128)(2,1)} copy(bf16[512,48,128]{2,1,0:T(8,128)(2,1)} %all-gather.3.cloned.1.call-done) | data formatting | bytes 12582912 | tf_op jit(solution)/shard_map/all_gather | solution.py:70
  187.5 13.3 %bitcast_reduce_fusion = (f32[32,48]{1,0:T(8,128)S(1)}, f32[128,48,32]{1,2,0:T(8,128)S(1)}) fusion(bf16[512,32,128]{1,0,2:T(8,128)(2,1)} %copy.37, bf16[512,48,128]{1,0,2:T(8,128)(2,1)} %copy.31), kind=kOutput, calls=%fused_computation.7 | convolution fusion | flops 201521664 | bytes 11278336 | tf_op jit(solution)/shard_map/kih,kjh->ijh/dot_general | solution.py:71
  201.2 1.2 copy-done.1
  203.1 1.8 multiply_convert_fusion
  204.9 10.8 %fusion.90 = bf16[128,512,32]{1,2,0:T(8,128)(2,1)} fusion(bf16[512,48,128]{1,0,2:T(8,128)(2,1)} %copy.31, bf16[32,48,128]{1,0,2:T(8,128)(2,1)S(1)} %get-tuple-element.8), kind=kOutput, calls=%fused_computation.132 | convolution fusion | flops 201326592 | bytes 10878976 | tf_op jit(solution)/shard_map/ijh,kjh->kih/dot_general | solution.py:91
  215.6 9.1 %copy.36 = bf16[128,512,32]{0,2,1:T(8,128)(2,1)} copy(bf16[128,512,32]{1,2,0:T(8,128)(2,1)} %fusion.90) | data formatting | bytes 8388608 | tf_op jit(solution)/shard_map/ijh,kjh->kih/dot_general | solution.py:91
  225.0 11.2 %fusion.91 = bf16[128,512,48]{1,2,0:T(8,128)(2,1)} fusion(bf16[512,32,128]{1,0,2:T(8,128)(2,1)} %copy.37, bf16[32,48,128]{1,0,2:T(8,128)(2,1)S(1)} %get-tuple-element.8), kind=kOutput, calls=%fused_computation.133 | convolution fusion | flops 201326592 | bytes 10878976 | tf_op jit(solution)/shard_map/ijh,kih->kjh/dot_general | solution.py:99
  236.3 9.8 %copy.38 = bf16[128,512,48]{0,2,1:T(8,128)(2,1)} copy(bf16[128,512,48]{1,2,0:T(8,128)(2,1)} %fusion.91) | data formatting | bytes 12582912 | tf_op jit(solution)/shard_map/ijh,kih->kjh/dot_general | solution.py:99
  246.1 1.2 copy-done.13
  250.7 1.7 fusion.26
  252.4 40.1 %reduce-scatter.3.cloned.1.call-done = bf16[32,32,128]{2,1,0:T(8,128)(2,1)} async-done(((bf16[512,32,128]{2,1,0:T(8,128)(2,1)}), bf16[32,32,128]{2,1,0:T(8,128)(2,1)}) %reduce-scatter.3.cloned.1.call-update) | async-done | bytes 262160 | tf_op jit(solution)/shard_map/reduce_scatter | solution.py:90
  292.4 1.2 fusion.54
  294.5 1.3 fusion.52
  295.8 104.1 %reduce-scatter.5.cloned.1.call-done = bf16[32,48,128]{2,1,0:T(8,128)(2,1)} async-done(((bf16[512,48,128]{2,1,0:T(8,128)(2,1)}), bf16[32,48,128]{2,1,0:T(8,128)(2,1)}) %reduce-scatter.5.cloned.1.call-update) | async-done | bytes 393232 | tf_op jit(solution)/shard_map/reduce_scatter | solution.py:98
  399.9 1.3 fusion.28
  402.2 1.7 fusion.19
  (85 shorter events, 14.0 us)
Async XLA Ops:
  7.2 6.9 %copy-start = (bf16[128,256]{1,0:T(8,128)(2,1)S(1)}, bf16[128,256]{1,0:T(8,128)(2,1)}, u32[]{:S(2)}) copy-start(bf16[128,256]{1,0:T(8,128)(2,1)} %param.18) | copy-start | bytes 196612
  7.2 6.0 %copy-start.10 = (bf16[32,48,128]{2,1,0:T(8,128)(2,1)S(1)}, bf16[32,48,128]{2,1,0:T(8,128)(2,1)}, u32[]{:S(2)}) copy-start(bf16[32,48,128]{2,1,0:T(8,128)(2,1)} %param.14) | copy-start | bytes 1179652
  7.2 78.0 %all-gather.5.cloned.1.call-start = ((), (), s32[]{:S(2)}) async-start(), calls=%async_computation.3 | async-start | bytes 4456448 | tf_op jit(solution)/shard_map/all_gather | solution.py:69
  8.5 5.6 %copy-start.19 = (f32[128]{0:T(128)S(1)}, f32[128]{0:T(128)}, u32[]{:S(2)}) copy-start(f32[128]{0:T(128)} %param.15) | copy-start | bytes 1540
  8.5 5.6 %copy-start.20 = (f32[128]{0:T(128)S(1)}, f32[128]{0:T(128)}, u32[]{:S(2)}) copy-start(f32[128]{0:T(128)} %param.16) | copy-start | bytes 1540
  13.2 151.3 %all-gather.3.cloned.1.call-start = ((), (), s32[]{:S(2)}) async-start(), calls=%async_computation.2 | async-start | bytes 6684672 | tf_op jit(solution)/shard_map/all_gather | solution.py:70
  14.1 3.0 copy-start.4
  14.7 1.2 copy-start.2
  15.8 2.6 copy-start.18
  16.8 275.6 %reduce-scatter.3.cloned.1.call-start = ((), (), s32[]{:S(2)}) async-start(), calls=%async_computation.4 | async-start | bytes 4456448 | tf_op jit(solution)/shard_map/reduce_scatter | solution.py:90
  17.9 1.8 copy-start.14
  17.9 1.7 copy-start.16
  17.9 1.7 copy-start.21
  200.8 1.6 copy-start.1
  224.8 175.2 %reduce-scatter.5.cloned.1.call-start = ((), (), s32[]{:S(2)}) async-start(), calls=%async_computation.5 | async-start | bytes 6684672 | tf_op jit(solution)/shard_map/reduce_scatter | solution.py:98
  246.1 1.2 copy-start.13
  246.1 2.3 copy-start.9
  246.1 3.3 copy-start.15
  248.4 1.6 copy-start.5
  249.9 42.6 %copy-start.7 = (f32[32,32,256]{2,1,0:T(8,128)S(1)}, f32[32,32,256]{2,1,0:T(8,128)}, u32[]{:S(2)}) copy-start(f32[32,32,256]{2,1,0:T(8,128)} %copy-done.6) | copy-start | bytes 3145732
  250.0 43.6 %copy-start.12 = (bf16[32,32,128]{2,1,0:T(8,128)(2,1)S(1)}, bf16[32,32,128]{2,1,0:T(8,128)(2,1)}, u32[]{:S(2)}) copy-start(bf16[32,32,128]{2,1,0:T(8,128)(2,1)} %param.13) | copy-start | bytes 786436
  250.0 43.6 %copy-start.17 = (bf16[128,256]{1,0:T(8,128)(2,1)S(1)}, bf16[128,256]{1,0:T(8,128)(2,1)}, u32[]{:S(2)}) copy-start(bf16[128,256]{1,0:T(8,128)(2,1)} %param.17) | copy-start | bytes 196612
  252.4 147.6 %copy-start.3 = (f32[32,48,256]{2,1,0:T(8,128)S(1)}, f32[32,48,256]{2,1,0:T(8,128)}, u32[]{:S(2)}) copy-start(f32[32,48,256]{2,1,0:T(8,128)} %copy-done.2) | copy-start | bytes 4718596
  294.5 106.8 %copy-start.11 = (bf16[32,48,128]{2,1,0:T(8,128)(2,1)S(1)}, bf16[32,48,128]{2,1,0:T(8,128)(2,1)}, u32[]{:S(2)}) copy-start(bf16[32,48,128]{2,1,0:T(8,128)(2,1)} %param.14) | copy-start | bytes 1179652
  (3 other events, 2.5 us)
Sparse Core Ops, SparseCore 0:
  13.3 71.8 all-gather.4
  88.4 75.9 all-gather.2
  224.9 67.4 reduce-scatter.2
  296.7 103.1 reduce-scatter.4
where the time goes:
time: 411 us; the launch traced here: 410 us
  waiting for transfers between devices  263 us (64%)
  local copies, waits for them, and re-layouts  74.8 us (18%)
  matrix products  41.3 us (10%)
  other arithmetic  16.9 us (4%)
  between operations  14.2 us (3%)
    reduce_scatter x1, waiting for transfers between devices, per_device(): lax.psum_scatter(jnp.einsum('ijh,kih->kjh', d_triangle, left_full, prefer...  104 us
    all_gather x1, waiting for transfers between devices, per_device(): left_full = lax.all_gather(left_gated, 'col', axis=0, tiled=True)  62.2 us
    all_gather x1, waiting for transfers between devices, per_device(): right_full = lax.all_gather(right_gated, 'row', axis=0, tiled=True)  56.2 us
    reduce_scatter x1, waiting for transfers between devices, per_device(): lax.psum_scatter(jnp.einsum('ijh,kjh->kih', d_triangle, right_full, prefe...  40.1 us
    all_gather x1, local copies, waits for them, and re-layouts, per_device(): right_full = lax.all_gather(right_gated, 'row', axis=0, tiled=True)  23.1 us
    all_gather x1, local copies, waits for them, and re-layouts, per_device(): left_full = lax.all_gather(left_gated, 'col', axis=0, tiled=True)  23 us
    dot_general x1, matrix products, per_device(): jnp.einsum('kih,kjh->ijh', left_full, right_full, preferred_element_type=...  13.3 us
    dot_general x1, matrix products, per_device(): jnp.einsum('ijh,kih->kjh', d_triangle, left_full, preferred_element_type=...  11.2 us
  transfers between devices with their start and end apart: 4, of which 4 were waited for; matrix products, arithmetic and copies ran while one was open for 15% of the time, Pallas kernels for 0%

commit v1 on v0

v1 whole, which is shorter than its diff:
```python
import jax
import jax.numpy as jnp
from jax import lax
from jax.experimental import pallas as pl
from jax.experimental.pallas import tpu as pltpu
from jax.sharding import PartitionSpec as P

MESH = pl.DeviceIdType.MESH
BF16 = jnp.bfloat16
F32 = jnp.float32
NZ = 8
PLANE = 32
HS = 4
EPS = 1e-05


def standardize(values):
    center = values - jnp.mean(values, axis=-1, keepdims=True)
    inverse = lax.rsqrt(jnp.mean(center * center, axis=-1, keepdims=True) + EPS)
    return center * inverse, inverse


def norm_back(upstream, standard, inverse, gain):
    scaled = upstream * gain
    return inverse * (
        scaled
        - jnp.mean(scaled, axis=-1, keepdims=True)
        - standard * jnp.mean(scaled * standard, axis=-1, keepdims=True)
    )


def dot_nn(a, b):
    return lax.dot_general(a, b, (((1,), (0,)), ((), ())), preferred_element_type=F32)


def dot_nt(a, b):
    return lax.dot_general(a, b, (((1,), (1,)), ((), ())), preferred_element_type=F32)


def swap64(x0, x1):
    low = lax.broadcasted_iota(jnp.int32, x0.shape, 1) < 64
    return (
        jnp.where(low, x0, pltpu.roll(x1, 64, 1)),
        jnp.where(low, pltpu.roll(x0, 64, 1), x1),
    )


def swap32(x0, x1):
    low = lax.broadcasted_iota(jnp.int32, x0.shape, 1) % 64 < 32
    return (
        jnp.where(low, x0, pltpu.roll(x1, 32, 1)),
        jnp.where(low, pltpu.roll(x0, 96, 1), x1),
    )


def exchange4(x):
    y0, y2 = swap64(x[0], x[2])
    y1, y3 = swap64(x[1], x[3])
    z0, z1 = swap32(y0, y1)
    z2, z3 = swap32(y2, y3)
    return z0, z1, z2, z3


def project_kernel(left, right, gain, bias, w_left, w_right, ls, rs, lpre, rpre, scr):
    g, bi = gain[...], bias[...]
    zeros = jnp.zeros((16, 128), F32)

    def rows_of(tile):
        standard, _ = standardize(tile.astype(F32))
        return standard * g + bi

    wl = w_left[...].T

    def left_step(a, _):
        normed = rows_of(jnp.concatenate([left[8 * b + a] for b in range(4)], axis=0))
        pre = dot_nt(wl, normed.astype(BF16))
        lpre[a] = pre
        scr[pl.ds(a, 128, stride=8), :] = jax.nn.sigmoid(pre[128:]) * pre[:128]
        return 0

    lax.fori_loop(0, 8, left_step, 0, unroll=2)
    ls[...] = scr[0:1024, :].astype(BF16).reshape(PLANE, 32, 128)

    wr = w_right[...].T

    def right_step(a, _):
        normed = rows_of(jnp.concatenate([right[a], right[16 + a]], axis=0))
        padded = jnp.concatenate([normed[:48], zeros, normed[48:], zeros], axis=0)
        pre = dot_nt(wr, padded.astype(BF16))
        rpre[a] = pre
        scr[pl.ds(a, 128, stride=16), :] = jax.nn.sigmoid(pre[128:]) * pre[:128]
        return 0

    lax.fori_loop(0, 16, right_step, 0, unroll=2)
    rs[...] = scr[...].astype(BF16).reshape(PLANE, 64, 128)


def project_back_kernel(dl, dr, left, right, lpre, rpre, gain, w_left, w_right, gl, gr, scr):
    g = gain[...]

    def back(d, pre, w, x):
        p, q = pre[:128], pre[128:]
        squash = jax.nn.sigmoid(q)
        d_pre = jnp.concatenate([d * squash, d * p * squash * (1.0 - squash)], axis=0)
        e = dot_nn(w, d_pre.astype(BF16)).T
        return e, x

    scr[0:1024, :] = dl[...].reshape(1024, 128).astype(F32)
    wl = w_left[...]

    def left_step(a, _):
        d = scr[pl.ds(a, 128, stride=8), :]
        x = jnp.concatenate([left[8 * b + a] for b in range(4)], axis=0).astype(F32)
        e, x = back(d, lpre[a], wl, x)
        standard, inverse = standardize(x)
        out = norm_back(e, standard, inverse, g).astype(BF16)
        for b in range(4):
            gl[8 * b + a] = out[32 * b : 32 * b + 32]
        return 0

    lax.fori_loop(0, 8, left_step, 0, unroll=2)

    scr[...] = dr[...].reshape(2048, 128).astype(F32)
    wr = w_right[...]

    def right_step(a, _):
        d = scr[pl.ds(a, 128, stride=16), :]
        x = jnp.concatenate([right[a], right[16 + a]], axis=0).astype(F32)
        e, x = back(d, rpre[a], wr, x)
        e = jnp.concatenate([e[0:48], e[64:112]], axis=0)
        standard, inverse = standardize(x)
        out = norm_back(e, standard, inverse, g).astype(BF16)
        gr[a] = out[:48]
        gr[16 + a] = out[48:]
        return 0

    lax.fori_loop(0, 16, right_step, 0, unroll=2)


FLOWS = ((1, 0, 4), (1, 1, 3), (-1, 0, 3), (-1, 1, 4))


def triangle_kernel(
    ls, rs, pair_out, cot, gain, bias, w_gate, w_out, o_gain, o_bias,
    result, grad_out, dl_out, dr_out,
    lbuf, rbuf, tsend, tbuf, dsend, dbuf, drsend, drbuf, dls, rsbuf, dlsend, dlbuf,
    lm, rm, dm, scr, big,
    a2a_send, a2a_recv, ag_send, ag_recv, rs_send, rs_recv,
):
    row = lax.axis_index("row")
    col = lax.axis_index("col")
    z = lax.rem(col, NZ)
    yl = col // NZ
    me = row * 2 + yl

    def plane_id(p):
        return {"row": p // 2, "col": lax.rem(p, 2) * NZ + z}

    def z_id(direction):
        return {"row": row, "col": yl * NZ + lax.rem(z + NZ + direction, NZ)}

    barrier = pltpu.get_barrier_semaphore()

    def greet(s, _):
        p = lax.rem(me + s, PLANE)
        pl.semaphore_signal(barrier, inc=1, device_id=plane_id(p), device_id_type=MESH)
        return 0

    lax.fori_loop(1, PLANE, greet, 0)
    for direction in (1, -1):
        pl.semaphore_signal(barrier, inc=1, device_id=z_id(direction), device_id_type=MESH)
    pl.semaphore_wait(barrier, PLANE - 1 + 2)

    def a2a_start(n, src, dst):
        pltpu.make_async_copy(src.at[me], dst.at[me], a2a_recv.at[n]).start()

        def send(s, _):
            p = lax.rem(me + s, PLANE)
            pltpu.make_async_remote_copy(
                src_ref=src.at[p], dst_ref=dst.at[me],
                send_sem=a2a_send.at[n], recv_sem=a2a_recv.at[n],
                device_id=plane_id(p), device_id_type=MESH,
            ).start()
            return 0

        lax.fori_loop(1, PLANE, send, 0)

    def a2a_wait(n, dst):
        pltpu.make_async_copy(dst, dst, a2a_recv.at[n]).wait()

    def a2a_drain(n, src):
        part = src.at[pl.ds(0, PLANE - 1)]
        pltpu.make_async_copy(part, part, a2a_send.at[n]).wait()

    def gather_copy(f, s):
        direction, half, _ = FLOWS[f]
        block = lbuf.at[lax.rem(z + NZ - direction * s, NZ), pl.ds(16 * half, 16)]
        return pltpu.make_async_remote_copy(
            src_ref=block, dst_ref=block,
            send_sem=ag_send.at[f, s], recv_sem=ag_recv.at[f, s],
            device_id=z_id(direction), device_id_type=MESH,
        )

    def unmix_left(zz):
        def step(n, _):
            ylk, q = n // 4, lax.rem(n, 4)
            x = [lbuf[zz, (4 * q + t) * 2 + ylk].astype(F32) for t in range(4)]
            y = exchange4(x)
            k0 = pl.multiple_of((ylk * NZ + zz) * 32, 32)
            lanes = pl.ds(pl.multiple_of(q * 128, 128), 128)
            for h in range(HS):
                block = jnp.concatenate([y[b][8 * h : 8 * h + 8] for b in range(4)], axis=0)
                lm[h, pl.ds(k0, 32), lanes] = block.astype(BF16)
            return 0

        lax.fori_loop(0, 8, step, 0)

    def unmix_pair(src, dst):
        def step(r, _):
            y = swap64(src[2 * r].astype(F32), src[2 * r + 1].astype(F32))
            r0 = pl.multiple_of(r * 32, 32)
            for h in range(HS):
                block = jnp.concatenate([y[g][16 * h : 16 * h + 16] for g in range(2)], axis=0)
                dst[h, pl.ds(r0, 32), :] = block.astype(BF16)
            return 0

        lax.fori_loop(0, 16, step, 0)

    def mix_pair(dst):
        def step(r, _):
            for h in range(HS):
                r0 = pl.multiple_of(h * 512 + r * 32, 32)
                y = swap64(scr[pl.ds(r0, 16), :], scr[pl.ds(r0 + 16, 16), :])
                for g in range(2):
                    dst[2 * r + g, 16 * h : 16 * h + 16, :] = y[g].astype(BF16)
            return 0

        lax.fori_loop(0, 16, step, 0)

    a2a_start(0, ls, lbuf.at[z])
    a2a_start(1, rs, rbuf)
    a2a_wait(0, lbuf.at[z])
    for f in range(4):
        gather_copy(f, 0).start()
    a2a_wait(1, rbuf)
    unmix_pair(rbuf, rm)
    unmix_left(z)
    for s in range(4):
        for f in range(4):
            if s < FLOWS[f][2]:
                gather_copy(f, s).wait_recv()
                if s + 1 < FLOWS[f][2]:
                    gather_copy(f, s + 1).start()
        if s < 3:
            unmix_left(lax.rem(z + NZ - s - 1, NZ))
            unmix_left(lax.rem(z + s + 1, NZ))
        else:
            unmix_left(lax.rem(z + 4, NZ))

    for h in range(HS):
        scr[512 * h : 512 * h + 512, :] = dot_nn(rm[h].T, lm[h]).T
    mix_pair(tsend)
    a2a_start(2, tsend, tbuf)
    a2a_wait(2, tbuf)

    scr[...] = tbuf[...].reshape(2048, 128).astype(F32)
    g_in, b_in, g_tri, b_tri = gain[...], bias[...], o_gain[...], o_bias[...]
    wg, wo = w_gate[...], w_out[...]
    zeros = jnp.zeros((16, 128), F32)

    def rows_step(a, _):
        tri = scr[pl.ds(a, 128, stride=16), :].T
        tri = jnp.concatenate([tri[0:48], tri[64:112]], axis=0)
        x = jnp.concatenate([pair_out[a], pair_out[16 + a]], axis=0).astype(F32)
        up = jnp.concatenate([cot[a], cot[16 + a]], axis=0).astype(F32)
        out_std, out_inv = standardize(x)
        gate = jax.nn.sigmoid(dot_nn((out_std * g_in + b_in).astype(BF16), wg))
        tri_std, tri_inv = standardize(tri)
        proj = dot_nn((tri_std * g_tri + b_tri).astype(BF16), wo)
        res = (gate * proj).astype(BF16)
        result[a] = res[:48]
        result[16 + a] = res[48:]
        d_proj = (up * gate).astype(BF16)
        d_gate = (up * proj * gate * (1.0 - gate)).astype(BF16)
        g_out = norm_back(dot_nt(d_gate, wg), out_std, out_inv, g_in).astype(BF16)
        grad_out[a] = g_out[:48]
        grad_out[16 + a] = g_out[48:]
        d_tri = norm_back(dot_nt(d_proj, wo), tri_std, tri_inv, g_tri)
        padded = jnp.concatenate([d_tri[:48], zeros, d_tri[48:], zeros], axis=0)
        scr[pl.ds(a, 128, stride=16), :] = padded.T
        return 0

    lax.fori_loop(0, 16, rows_step, 0)
    dsend[...] = scr[...].astype(BF16).reshape(PLANE, 64, 128)
    a2a_start(3, dsend, dbuf)
    a2a_wait(3, dbuf)
    unmix_pair(dbuf, dm)

    for h in range(HS):
        big[h] = dot_nt(rm[h], dm[h])

    def pack_left(c, _):
        k0 = pl.multiple_of(c * 32, 32)
        for q in range(4):
            x = [
                jnp.concatenate(
                    [big[h, pl.ds(k0 + 8 * b, 8), 128 * q : 128 * q + 128] for h in range(HS)],
                    axis=0,
                )
                for b in range(4)
            ]
            y = exchange4(x)
            for t in range(4):
                dls[lax.rem(c, NZ), (4 * q + t) * 2 + c // NZ] = y[t].astype(BF16)
        return 0

    lax.fori_loop(0, 16, pack_left, 0)

    def sum_copy(f, s):
        direction, half, steps = FLOWS[f]
        block = dls.at[lax.rem(z + NZ + direction * (steps - s), NZ), pl.ds(16 * half, 16)]
        return pltpu.make_async_remote_copy(
            src_ref=block, dst_ref=rsbuf.at[f, s],
            send_sem=rs_send.at[f, s], recv_sem=rs_recv.at[f, s],
            device_id=z_id(direction), device_id_type=MESH,
        )

    for f in range(4):
        sum_copy(f, 0).start()

    for h in range(HS):
        scr[512 * h : 512 * h + 512, :] = dot_nn(lm[h], dm[h])
    mix_pair(drsend)
    a2a_start(4, drsend, drbuf)

    for s in range(4):
        for f in range(4):
            direction, half, steps = FLOWS[f]
            if s < steps:
                sum_copy(f, s).wait_recv()
                if s + 1 < steps:
                    chunk = lax.rem(z + NZ + direction * (steps - s - 1), NZ)
                    here = (chunk, pl.ds(16 * half, 16))
                    dls[here] = (dls[here].astype(F32) + rsbuf[f, s].astype(F32)).astype(BF16)
                    sum_copy(f, s + 1).start()
    for half in range(2):
        here = pl.ds(16 * half, 16)
        total = dls[z, here].astype(F32)
        for f in range(4):
            if FLOWS[f][1] == half:
                total = total + rsbuf[f, FLOWS[f][2] - 1].astype(F32)
        dlsend[here] = total.astype(BF16)
    a2a_start(5, dlsend, dlbuf)
    a2a_wait(4, drbuf)
    dr_out[...] = drbuf[...]
    a2a_wait(5, dlbuf)
    dl_out[...] = dlbuf[...]

    for n, src in enumerate((ls, rs, tsend, dsend, drsend, dlsend)):
        a2a_drain(n, src)
    for f in range(4):
        for s in range(FLOWS[f][2]):
            gather_copy(f, s).wait_send()
            sum_copy(f, s).wait_send()


VMEM_LIMIT = 56 * 1024 * 1024


def per_device(
    pair_out, pair_left, pair_right, ln_gain, ln_bias, w_left, w_right, w_gate, w_out,
    out_gain, out_bias, cotangent,
):
    vm = pl.BlockSpec(memory_space=pltpu.VMEM)
    gain, bias = ln_gain.reshape(1, 128), ln_bias.reshape(1, 128)
    o_gain, o_bias = out_gain.reshape(1, 128), out_bias.reshape(1, 128)
    ls, rs, lpre, rpre = pl.pallas_call(
        project_kernel,
        out_shape=(
            jax.ShapeDtypeStruct((PLANE, 32, 128), BF16),
            jax.ShapeDtypeStruct((PLANE, 64, 128), BF16),
            jax.ShapeDtypeStruct((8, 256, 128), F32),
            jax.ShapeDtypeStruct((16, 256, 128), F32),
        ),
        in_specs=[vm] * 6,
        out_specs=(vm,) * 4,
        scratch_shapes=[pltpu.VMEM((2048, 128), F32)],
        compiler_params=pltpu.CompilerParams(vmem_limit_bytes=VMEM_LIMIT),
        name="project",
    )(pair_left, pair_right, gain, bias, w_left, w_right)

    half_slots = pltpu.VMEM((PLANE, 32, 128), BF16)
    slots = pltpu.VMEM((PLANE, 64, 128), BF16)
    dma = pltpu.SemaphoreType.DMA
    result, grad_out, dl, dr = pl.pallas_call(
        triangle_kernel,
        out_shape=(
            jax.ShapeDtypeStruct((32, 48, 128), BF16),
            jax.ShapeDtypeStruct((32, 48, 128), BF16),
            jax.ShapeDtypeStruct((PLANE, 32, 128), BF16),
            jax.ShapeDtypeStruct((PLANE, 64, 128), BF16),
        ),
        in_specs=[vm] * 10,
        out_specs=(vm,) * 4,
        scratch_shapes=[
            pltpu.VMEM((NZ, PLANE, 32, 128), BF16),
            slots,
            slots,
            slots,
            slots,
            slots,
            slots,
            slots,
            pltpu.VMEM((NZ, PLANE, 32, 128), BF16),
            pltpu.VMEM((4, 4, 16, 32, 128), BF16),
            half_slots,
            half_slots,
            pltpu.VMEM((HS, 512, 512), BF16),
            pltpu.VMEM((HS, 512, 128), BF16),
            pltpu.VMEM((HS, 512, 128), BF16),
            pltpu.VMEM((2048, 128), F32),
            pltpu.VMEM((HS, 512, 512), F32),
            dma((6,)), dma((6,)), dma((4, 4)), dma((4, 4)), dma((4, 4)), dma((4, 4)),
        ],
        compiler_params=pltpu.CompilerParams(
            vmem_limit_bytes=VMEM_LIMIT, collective_id=0, has_side_effects=True
        ),
        name="triangle",
    )(ls, rs, pair_out, cotangent, gain, bias, w_gate, w_out, o_gain, o_bias)

    grad_left, grad_right = pl.pallas_call(
        project_back_kernel,
        out_shape=(
            jax.ShapeDtypeStruct((32, 32, 128), BF16),
            jax.ShapeDtypeStruct((32, 48, 128), BF16),
        ),
        in_specs=[vm] * 9,
        out_specs=(vm,) * 2,
        scratch_shapes=[pltpu.VMEM((2048, 128), F32)],
        compiler_params=pltpu.CompilerParams(vmem_limit_bytes=VMEM_LIMIT),
        name="project_back",
    )(dl, dr, pair_left, pair_right, lpre, rpre, gain, w_left, w_right)
    return result, grad_out, grad_left, grad_right


def solution(mesh):
    pairs, lefts = P("row", "col", None), P("col", "row", None)
    return jax.shard_map(
        per_device,
        mesh=mesh,
        in_specs=(pairs, lefts, pairs, P(), P(), P(), P(), P(), P(), P(), P(), pairs),
        out_specs=(pairs, pairs, lefts, pairs),
        check_vma=False,
    )
```

time: 411 us -> 132 us (0.32)
  waiting for transfers between devices: 263 us -> 0 us
  Pallas kernels: 0 us -> 130 us
  local copies, waits for them, and re-layouts: 74.8 us -> 1.5 us
  matrix products: 41.3 us -> 0 us
  other arithmetic: 16.9 us -> 0 us
  between operations: 14.2 us -> 0.66 us
    reduce_scatter x2 -> x0, waiting for transfers between devices: 144 us -> none  [the longest x1 104 us: per_device(): lax.psum_scatter(jnp.einsum('ijh,kih->kjh', d_triangle, left_full, prefer...]
    pallas_call x0 -> x3, Pallas kernels: none -> 130 us  [the longest x1 114 us: per_device(): pl.pallas_call(triangle_kernel, out_shape=(jax.ShapeDtypeStruct((32, 48,...]
    all_gather x2 -> x0, waiting for transfers between devices: 118 us -> none  [the longest x1 62.2 us: per_device(): left_full = lax.all_gather(left_gated, 'col', axis=0, tiled=True)]
    all_gather x2 -> x0, local copies, waits for them, and re-layouts: 46.1 us -> none  [the longest x1 23.1 us: per_device(): right_full = lax.all_gather(right_gated, 'row', axis=0, tiled=True)]
    dot_general x11 -> x0, matrix products: 41.3 us -> none  [the longest x1 13.3 us: per_device(): jnp.einsum('kih,kjh->ijh', left_full, right_full, preferred_element_type=...]
    dot_general x2 -> x0, local copies, waits for them, and re-layouts: 18.9 us -> none  [the longest x1 9.8 us: per_device(): jnp.einsum('ijh,kih->kjh', d_triangle, left_full, preferred_element_type=...]
    convert_element_type x7 -> x0, other arithmetic: 8.69 us -> none  [the longest x2 2.97 us: project_back(): norm_back(d_normed.reshape(standard.shape), standard, inverse, gain)]
    reduce_sum x9 -> x0, other arithmetic: 5.59 us -> none  [the longest x4 2.68 us: normalize(): jnp.mean(center * center, axis=-1, keepdims=True) + 1e-05]
  transfers between devices with their start and end apart: 4 -> 0, of which waited for: 4 -> 0; matrix products, arithmetic and copies ran while one was open for 15% -> 0% of each run, Pallas kernels for 0% -> 0%
where the time goes in v1:
time: 132 us
  Pallas kernels  130 us (98%)
  local copies, waits for them, and re-layouts  1.5 us (1%)
    pallas_call x1, Pallas kernels, per_device(): pl.pallas_call(triangle_kernel, out_shape=(jax.ShapeDtypeStruct((32, 48,...  114 us
    pallas_call x1, Pallas kernels, per_device(): pl.pallas_call(project_back_kernel, out_shape=(jax.ShapeDtypeStruct((32,...  8.52 us
    pallas_call x1, Pallas kernels, per_device(): pl.pallas_call(project_kernel, out_shape=(jax.ShapeDtypeStruct((PLANE, 32...  7.87 us

profile of v1, /device:TPU:1, one launch (start us, length us, event | category | flops | bytes accessed | tf_op | source)
XLA Modules:
  0.0 132.2 jit_solution(4113551458459508206)
XLA Ops:
  0.6 7.9 %project.1 = (bf16[32,32,128]{2,1,0:T(8,128)(2,1)}, bf16[32,64,128]{2,1,0:T(8,128)(2,1)}, f32[8,256,128]{2,1,0:T(8,128)}, f32[16,256,128]{2,1,0:T(8,128)}) custom-call(bf16[32,32,128]{2,1,0:T(8,128)(2,1)} %left.3, bf16[32,48,128]{2,1,0:T(8,128)(2,1)} %right.3, f32[1,128]{1,0:T(1,128)} %bitcast.4, f32[1,128]{1,0:T(1,128)} %bitcast.7, ...), custom_call_target="tpu_custom_call" | custom-call | tf_op jit(solution)/shard_map/project/pallas_call | solution.py:377
  8.5 113.7 %triangle.1 = (bf16[32,48,128]{2,1,0:T(8,128)(2,1)}, bf16[32,48,128]{2,1,0:T(8,128)(2,1)}, bf16[32,32,128]{2,1,0:T(8,128)(2,1)}, bf16[32,64,128]{2,1,0:T(8,128)(2,1)}) custom-call(bf16[32,32,128]{2,1,0:T(8,128)(2,1)} %get-tuple-element.14.ls, bf16[32,64,128]{2,1,0:T(8,128)(2,1)} %get-tuple-element.15.rs, bf16[32,48,128]{2,1,0:T(8,128)(2,1)} %pair_out.1, ...), custom_call_target="tpu_custom_call" | custom-call | tf_op jit(solution)/shard_map/triangle/pallas_call | solution.py:395
  122.2 0.0 copy-start.1
  122.2 0.0 copy-start
  122.2 8.5 %project_back.1 = (bf16[32,32,128]{2,1,0:T(8,128)(2,1)}, bf16[32,48,128]{2,1,0:T(8,128)(2,1)}) custom-call(bf16[32,32,128]{2,1,0:T(8,128)(2,1)} %get-tuple-element.18.dl, bf16[32,64,128]{2,1,0:T(8,128)(2,1)} %get-tuple-element.19.dr, bf16[32,32,128]{2,1,0:T(8,128)(2,1)} %left.3, bf16[32,48,128]{2,1,0:T(8,128)(2,1)} %right.3, ...), custom_call_target="tpu_custom_call" | custom-call | tf_op jit(solution)/shard_map/project_back/pallas_call | solution.py:431
  130.7 0.0 copy-done.1
  130.7 0.7 copy.18
  131.5 0.0 copy-done
  131.5 0.7 copy.19
Async XLA Ops:
  122.2 8.5 %copy-start.1 = (bf16[32,48,128]{2,1,0:T(8,128)(2,1)S(1)}, bf16[32,48,128]{2,1,0:T(8,128)(2,1)}, u32[]{:S(2)}) copy-start(bf16[32,48,128]{2,1,0:T(8,128)(2,1)} %get-tuple-element.28) | copy-start | bytes 1179652
  122.2 9.3 %copy-start = (bf16[32,48,128]{2,1,0:T(8,128)(2,1)S(1)}, bf16[32,48,128]{2,1,0:T(8,128)(2,1)}, u32[]{:S(2)}) copy-start(bf16[32,48,128]{2,1,0:T(8,128)(2,1)} %get-tuple-element.29) | copy-start | bytes 1179652

commit v2 on v0

v2 whole, which is shorter than its diff:
```python
import jax
import jax.numpy as jnp
from jax import lax
from jax.experimental import pallas as pl
from jax.experimental.pallas import tpu as pltpu
from jax.sharding import PartitionSpec as P

MESH = pl.DeviceIdType.MESH
BF16 = jnp.bfloat16
F32 = jnp.float32
NZ = 8
PLANE = 32
HALF = PLANE // 2
HS = 4
EPS = 1e-05


def cat(parts, axis=0):
    return jnp.concatenate(parts, axis=axis)


def standardize(values):
    center = values - jnp.mean(values, axis=-1, keepdims=True)
    inverse = lax.rsqrt(jnp.mean(center * center, axis=-1, keepdims=True) + EPS)
    return center * inverse, inverse


def norm_back(upstream, standard, inverse, gain):
    scaled = upstream * gain
    return inverse * (
        scaled
        - jnp.mean(scaled, axis=-1, keepdims=True)
        - standard * jnp.mean(scaled * standard, axis=-1, keepdims=True)
    )


def dot_nn(a, b):
    return lax.dot_general(a, b, (((1,), (0,)), ((), ())), preferred_element_type=F32)


def dot_nt(a, b):
    return lax.dot_general(a, b, (((1,), (1,)), ((), ())), preferred_element_type=F32)


def swap64(x0, x1):
    low = lax.broadcasted_iota(jnp.int32, x0.shape, 1) < 64
    return (
        jnp.where(low, x0, pltpu.roll(x1, 64, 1)),
        jnp.where(low, pltpu.roll(x0, 64, 1), x1),
    )


def swap32(x0, x1):
    low = lax.broadcasted_iota(jnp.int32, x0.shape, 1) % 64 < 32
    return (
        jnp.where(low, x0, pltpu.roll(x1, 32, 1)),
        jnp.where(low, pltpu.roll(x0, 96, 1), x1),
    )


def exchange4(x):
    y0, y2 = swap64(x[0], x[2])
    y1, y3 = swap64(x[1], x[3])
    z0, z1 = swap32(y0, y1)
    z2, z3 = swap32(y2, y3)
    return z0, z1, z2, z3


def project_left(left, g, bi, w, ls, lpre, scr):
    x = cat([left[8 * b + a] for a in range(8) for b in range(4)]).astype(F32)
    standard, _ = standardize(x)
    pre = dot_nt(w.T, (standard * g + bi).astype(BF16))
    gated = jax.nn.sigmoid(pre[128:]) * pre[:128]
    for a in range(8):
        lpre[a] = pre[:, 128 * a : 128 * a + 128]
        scr[pl.ds(a, 128, stride=8), :] = gated[:, 128 * a : 128 * a + 128]
    ls[...] = scr[0:1024, :].astype(BF16).reshape(PLANE, 32, 128)


def project_right(right, g, bi, w, rs, rpre, scr):
    zeros = jnp.zeros((16, 128), F32)
    wr = w.T

    def step(n, _):
        x = cat([right[16 * b + n * 8 + t] for t in range(8) for b in range(2)]).astype(F32)
        standard, _ = standardize(x)
        normed = standard * g + bi
        normed = cat([y for t in range(16) for y in (normed[48 * t : 48 * t + 48], zeros)])
        pre = dot_nt(wr, normed.astype(BF16))
        gated = jax.nn.sigmoid(pre[128:]) * pre[:128]
        for t in range(8):
            rpre[n * 8 + t] = pre[:, 128 * t : 128 * t + 128]
            scr[pl.ds(n * 8 + t, 128, stride=16), :] = gated[:, 128 * t : 128 * t + 128]
        return 0

    lax.fori_loop(0, 2, step, 0)
    rs[...] = scr[...].astype(BF16).reshape(PLANE, 64, 128)


def gate_rows(pair_out, g, bi, wg, gate_s, std_s, inv_s):
    def step(n, _):
        x = cat([pair_out[16 * b + n * 8 + t] for t in range(8) for b in range(2)]).astype(F32)
        standard, inverse = standardize(x)
        rows = pl.ds(pl.multiple_of(n * 768, 768), 768)
        gate_s[rows, :] = jax.nn.sigmoid(dot_nn((standard * g + bi).astype(BF16), wg))
        std_s[rows, :] = standard
        inv_s[rows, :] = jnp.broadcast_to(inverse, standard.shape)
        return 0

    lax.fori_loop(0, 2, step, 0)


def slab_rows(n, scr, scr2, cot, g_in, g_tri, b_tri, wg, wo, gate_s, std_s, inv_s, result, grad_out):
    zeros = jnp.zeros((16, 128), F32)
    parts = []
    for t in range(8):
        tri = scr[pl.ds(n * 8 + t, 128, stride=16), :].T
        parts += [tri[0:48], tri[64:112]]
    tri = cat(parts)
    up = cat([cot[16 * b + n * 8 + t] for t in range(8) for b in range(2)]).astype(F32)
    rows = pl.ds(n * 768, 768)
    gate, out_std, out_inv = gate_s[rows, :], std_s[rows, :], inv_s[rows, :]
    tri_std, tri_inv = standardize(tri)
    proj = dot_nn((tri_std * g_tri + b_tri).astype(BF16), wo)
    gated_up = up * gate
    d_tri = norm_back(dot_nt(gated_up.astype(BF16), wo), tri_std, tri_inv, g_tri)
    res = (gate * proj).astype(BF16)
    d_gate = (gated_up * proj * (1.0 - gate)).astype(BF16)
    g_out = norm_back(dot_nt(d_gate, wg), out_std, out_inv, g_in).astype(BF16)
    for t in range(8):
        for b in range(2):
            o = (2 * t + b) * 48
            result[16 * b + n * 8 + t] = res[o : o + 48]
            grad_out[16 * b + n * 8 + t] = g_out[o : o + 48]
        o = 96 * t
        padded = cat([d_tri[o : o + 48], zeros, d_tri[o + 48 : o + 96], zeros])
        scr2[pl.ds(n * 8 + t, 128, stride=16), :] = padded.T


def d_pre_of(d, pre):
    p, q = pre[:128], pre[128:]
    squash = jax.nn.sigmoid(q)
    d_p = d * squash
    return cat([d_p, d_p * p * (1.0 - squash)]).astype(BF16)


def back_left(left, lpre, g, w, gl, scr):
    d = cat([scr[pl.ds(a, 128, stride=8), :] for a in range(8)], axis=1)
    pre = cat([lpre[a] for a in range(8)], axis=1)
    e = dot_nn(w, d_pre_of(d, pre)).T
    x = cat([left[8 * b + a] for a in range(8) for b in range(4)]).astype(F32)
    standard, inverse = standardize(x)
    out = norm_back(e, standard, inverse, g).astype(BF16)
    for a in range(8):
        for b in range(4):
            o = 128 * a + 32 * b
            gl[8 * b + a] = out[o : o + 32]


def back_right(n, right, rpre, g, w, gr, scr):
    d = cat([scr[pl.ds(n * 8 + t, 128, stride=16), :] for t in range(8)], axis=1)
    pre = cat([rpre[n * 8 + t] for t in range(8)], axis=1)
    e = dot_nn(w, d_pre_of(d, pre)).T
    e = cat([y for t in range(8) for y in (e[128 * t : 128 * t + 48], e[128 * t + 64 : 128 * t + 112])])
    x = cat([right[16 * b + n * 8 + t] for t in range(8) for b in range(2)]).astype(F32)
    standard, inverse = standardize(x)
    out = norm_back(e, standard, inverse, g).astype(BF16)
    for t in range(8):
        for b in range(2):
            o = (2 * t + b) * 48
            gr[16 * b + n * 8 + t] = out[o : o + 48]


FLOWS = ((1, 0, 4), (1, 1, 3), (-1, 0, 3), (-1, 1, 4))
QUART = HALF // 2


def triangle_kernel(
    left_hbm, right_hbm, out_hbm, cot_hbm, gain, bias, w_left, w_right, w_gate, w_out, o_gain, o_bias,
    result_hbm, grad_out_hbm, grad_left_hbm, grad_right_hbm,
    left, right, pair_out, cot, result, grad_out, grad_left, grad_right,
    ls, rs, lpre, rpre, gate_s, std_s, inv_s,
    lbuf, rbuf, tsend, tbuf, dsend, dbuf, drsend, drbuf, dls, rsbuf, dlsend, dlbuf,
    lm, rm, rmt, dm, scr, scr2, big,
    in_sem, out_sem, a2a_send, a2a_recv, ag_send, ag_recv, rs_send, rs_recv,
):
    row = lax.axis_index("row")
    col = lax.axis_index("col")
    z = lax.rem(col, NZ)
    yl = col // NZ
    core = lax.rem(row, 2)
    me16 = (row // 2) * 2 + yl
    me = core * HALF + me16

    def plane_id(p):
        q = lax.rem(p, HALF)
        return {"row": (q // 2) * 2 + p // HALF, "col": lax.rem(q, 2) * NZ + z}

    def z_id(direction):
        return {"row": row, "col": yl * NZ + lax.rem(z + NZ + direction, NZ)}

    barrier = pltpu.get_barrier_semaphore()

    def greet(s, _):
        p = lax.rem(me + s, PLANE)
        pl.semaphore_signal(barrier, inc=1, device_id=plane_id(p), device_id_type=MESH)
        return 0

    lax.fori_loop(1, PLANE, greet, 0)
    for direction in (1, -1):
        pl.semaphore_signal(barrier, inc=1, device_id=z_id(direction), device_id_type=MESH)

    loads = [
        pltpu.make_async_copy(src, dst, in_sem.at[n])
        for n, (src, dst) in enumerate(
            ((left_hbm, left), (right_hbm, right), (out_hbm, pair_out), (cot_hbm, cot))
        )
    ]
    stores = [
        pltpu.make_async_copy(src, dst, out_sem.at[n])
        for n, (src, dst) in enumerate(
            (
                (result, result_hbm),
                (grad_out, grad_out_hbm),
                (grad_left, grad_left_hbm),
                (grad_right, grad_right_hbm),
            )
        )
    ]
    for load in loads:
        load.start()

    def remote(n, src, dst, p):
        return pltpu.make_async_remote_copy(
            src_ref=src, dst_ref=dst.at[me],
            send_sem=a2a_send.at[n], recv_sem=a2a_recv.at[n],
            device_id=plane_id(p), device_id_type=MESH,
        )

    def all_start(n, src, dst, slot):
        pltpu.make_async_copy(src.at[me], dst.at[slot], a2a_recv.at[n]).start()

        def send(s, _):
            p = lax.rem(me + s, PLANE)
            pltpu.make_async_remote_copy(
                src_ref=src.at[p], dst_ref=dst.at[slot],
                send_sem=a2a_send.at[n], recv_sem=a2a_recv.at[n],
                device_id=plane_id(p), device_id_type=MESH,
            ).start()
            return 0

        lax.fori_loop(1, PLANE, send, 0)

    def all_drain(n, src):
        part = src.at[pl.ds(0, PLANE - 1)]
        pltpu.make_async_copy(part, part, a2a_send.at[n]).wait()

    def part_start(n, kappa, src, dst):
        @pl.when(core == kappa)
        def _():
            pltpu.make_async_copy(src.at[me16], dst.at[me], a2a_recv.at[n]).start()

        @pl.when(core != kappa)
        def _():
            remote(n, src.at[me16], dst, kappa * HALF + me16).start()

        def send(s, _):
            d = lax.rem(me16 + s, HALF)
            remote(n, src.at[d], dst, kappa * HALF + d).start()
            return 0

        lax.fori_loop(1, HALF, send, 0)

    def part_drain(n, kappa, src):
        @pl.when(core == kappa)
        def _():
            part = src.at[pl.ds(0, HALF - 1)]
            pltpu.make_async_copy(part, part, a2a_send.at[n]).wait()

        @pl.when(core != kappa)
        def _():
            pltpu.make_async_copy(src, src, a2a_send.at[n]).wait()

    def arrived(n, dst):
        pltpu.make_async_copy(dst, dst, a2a_recv.at[n]).wait()

    def z_slots(kappa, half):
        return pl.ds(HALF * kappa + QUART * half, QUART)

    def gather_copy(kappa, f, s):
        direction, half, _ = FLOWS[f]
        block = lbuf.at[lax.rem(z + NZ - direction * s, NZ), z_slots(kappa, half)]
        return pltpu.make_async_remote_copy(
            src_ref=block, dst_ref=block,
            send_sem=ag_send.at[kappa, f, s], recv_sem=ag_recv.at[kappa, f, s],
            device_id=z_id(direction), device_id_type=MESH,
        )

    def gather_start(kappa):
        for f in range(4):
            gather_copy(kappa, f, 0).start()

    def gather_pump(kappa, s):
        for f in range(4):
            if s < FLOWS[f][2]:
                gather_copy(kappa, f, s).wait_recv()
                if s + 1 < FLOWS[f][2]:
                    gather_copy(kappa, f, s + 1).start()

    def unmix_left(kappa, zz):
        def step(n, _):
            ylk, q = n // 2, lax.rem(n, 2)
            x = [lbuf[zz, HALF * kappa + (4 * q + t) * 2 + ylk].astype(F32) for t in range(4)]
            y = exchange4(x)
            k0 = pl.multiple_of((ylk * NZ + zz) * 32, 32)
            lanes = pl.ds(pl.multiple_of(256 * kappa + q * 128, 128), 128)
            for h in range(HS):
                block = cat([y[b][8 * h : 8 * h + 8] for b in range(4)])
                lm[h, pl.ds(k0, 32), lanes] = block.astype(BF16)
            return 0

        lax.fori_loop(0, 4, step, 0, unroll=2)

    def unmix_gathered(kappa, s):
        if s < 3:
            unmix_left(kappa, lax.rem(z + NZ - s - 1, NZ))
            unmix_left(kappa, lax.rem(z + s + 1, NZ))
        else:
            unmix_left(kappa, lax.rem(z + 4, NZ))

    def unmix_pair(src, first, count, put):
        def step(m, _):
            y = swap64(src[first + 2 * m].astype(F32), src[first + 2 * m + 1].astype(F32))
            for h in range(HS):
                put(h, m, cat([y[g][16 * h : 16 * h + 16] for g in range(2)]).astype(BF16))
            return 0

        lax.fori_loop(0, count, step, 0, unroll=2)

    def unmix_right():
        for kappa in range(2):

            def put(h, m, block):
                rm[h, pl.ds(pl.multiple_of((2 * m + kappa) * 32, 32), 32), :] = block

            unmix_pair(rbuf, HALF * kappa, 8, put)

    def unmix_d(kappa):
        def put(h, m, block):
            dm[h, pl.ds(pl.multiple_of(256 * kappa + m * 32, 32), 32), :] = block

        unmix_pair(dbuf, HALF * kappa, 8, put)

    def mix_pair(per_channel, blocks, put):
        def step(m, _):
            for h in range(HS):
                r0 = pl.multiple_of(h * per_channel + m * 32, 32)
                y = swap64(scr[pl.ds(r0, 16), :], scr[pl.ds(r0 + 16, 16), :])
                for v in range(2):
                    put(m, v, h, y[v].astype(BF16))
            return 0

        lax.fori_loop(0, blocks, step, 0, unroll=2)

    def triangle(kappa):
        for h in range(HS):
            scr[256 * h : 256 * h + 256, :] = dot_nn(rmt[h], lm[h, :, 256 * kappa : 256 * kappa + 256]).T

        def put(m, v, h, block):
            tsend[kappa, 2 * m + v, 16 * h : 16 * h + 16, :] = block

        mix_pair(256, 8, put)
        part_start(2 + kappa, kappa, tsend.at[kappa], tbuf)

    g_in, b_in, g_tri, b_tri = gain[...], bias[...], o_gain[...], o_bias[...]
    wg, wo = w_gate[...], w_out[...]

    def slab(kappa, n):
        @pl.when(core == kappa)
        def _():
            if n == 0:
                arrived(2 + kappa, tbuf)
                scr[...] = tbuf[...].reshape(2048, 128).astype(F32)
            slab_rows(
                n, scr, scr2, cot, g_in, g_tri, b_tri, wg, wo, gate_s, std_s, inv_s, result, grad_out
            )
            if n == 1:
                dsend[...] = scr2[...].astype(BF16).reshape(PLANE, 64, 128)
                all_start(4 + kappa, dsend, dbuf, me)
                stores[0].start()
                stores[1].start()

    def sum_copy(kappa, f, s):
        direction, half, steps = FLOWS[f]
        block = dls.at[lax.rem(z + NZ + direction * (steps - s), NZ), z_slots(kappa, half)]
        return pltpu.make_async_remote_copy(
            src_ref=block, dst_ref=rsbuf.at[kappa, f, s],
            send_sem=rs_send.at[kappa, f, s], recv_sem=rs_recv.at[kappa, f, s],
            device_id=z_id(direction), device_id_type=MESH,
        )

    def left_sums(kappa):
        arrived(4 + kappa, dbuf.at[pl.ds(HALF * kappa, HALF)])
        unmix_d(kappa)
        for h in range(HS):
            big[h] = dot_nt(rm[h], dm[h, 256 * kappa : 256 * kappa + 256, :])

        def pack(c, _):
            k0 = pl.multiple_of(c * 32, 32)
            for q in range(2):
                x = [
                    cat([big[h, pl.ds(k0 + 8 * b, 8), 128 * q : 128 * q + 128] for h in range(HS)])
                    for b in range(4)
                ]
                y = exchange4(x)
                for t in range(4):
                    slot = HALF * kappa + (4 * q + t) * 2 + c // NZ
                    dls[lax.rem(c, NZ), slot] = y[t].astype(BF16)
            return 0

        lax.fori_loop(0, 16, pack, 0, unroll=2)
        for f in range(4):
            sum_copy(kappa, f, 0).start()

    def sum_pump(kappa, s):
        for f in range(4):
            direction, half, steps = FLOWS[f]
            if s < steps:
                sum_copy(kappa, f, s).wait_recv()
                if s + 1 < steps:
                    here = (lax.rem(z + NZ + direction * (steps - s - 1), NZ), z_slots(kappa, half))
                    dls[here] = (dls[here].astype(F32) + rsbuf[kappa, f, s].astype(F32)).astype(BF16)
                    sum_copy(kappa, f, s + 1).start()

    def left_out(kappa):
        for half in range(2):
            total = dls[z, z_slots(kappa, half)].astype(F32)
            for f in range(4):
                if FLOWS[f][1] == half:
                    total = total + rsbuf[kappa, f, FLOWS[f][2] - 1].astype(F32)
            dlsend[kappa, QUART * half : QUART * half + QUART] = total.astype(BF16)
        part_start(7 + kappa, kappa, dlsend.at[kappa], dlbuf)

    loads[0].wait()
    project_left(left, g_in, b_in, w_left[...], ls, lpre, scr)
    pl.semaphore_wait(barrier, PLANE - 1 + 2)
    all_start(0, ls, lbuf.at[z], me)
    loads[1].wait()
    project_right(right, g_in, b_in, w_right[...], rs, rpre, scr2)
    all_start(1, rs, rbuf, me)
    arrived(0, lbuf.at[z])
    gather_start(0)
    loads[2].wait()
    gate_rows(pair_out, g_in, b_in, wg, gate_s, std_s, inv_s)
    unmix_left(0, z)
    unmix_left(1, z)
    gather_pump(0, 0)
    unmix_gathered(0, 0)
    arrived(1, rbuf)
    gather_pump(0, 1)
    unmix_right()
    for h in range(HS):
        rmt[h] = rm[h].T
    unmix_gathered(0, 1)
    gather_pump(0, 2)
    gather_start(1)
    unmix_gathered(0, 2)
    gather_pump(0, 3)
    unmix_gathered(0, 3)
    loads[3].wait()

    triangle(0)
    gather_pump(1, 0)
    unmix_gathered(1, 0)
    gather_pump(1, 1)
    unmix_gathered(1, 1)
    slab(0, 0)
    gather_pump(1, 2)
    unmix_gathered(1, 2)
    slab(0, 1)
    gather_pump(1, 3)
    unmix_gathered(1, 3)
    triangle(1)

    left_sums(0)
    slab(1, 0)
    sum_pump(0, 0)
    slab(1, 1)
    sum_pump(0, 1)
    sum_pump(0, 2)
    left_sums(1)
    sum_pump(0, 3)
    left_out(0)

    for h in range(HS):
        scr[512 * h : 512 * h + 512, :] = dot_nn(lm[h], dm[h])

    def put_right(m, v, h, block):
        drsend[lax.rem(m, 2) * HALF + (m // 2) * 2 + v, 16 * h : 16 * h + 16, :] = block

    mix_pair(512, 16, put_right)
    all_start(6, drsend, drbuf, me)
    sum_pump(1, 0)
    sum_pump(1, 1)
    arrived(6, drbuf)
    scr[...] = drbuf[...].reshape(2048, 128).astype(F32)
    wr = w_right[...]
    back_right(0, right, rpre, g_in, wr, grad_right, scr)
    sum_pump(1, 2)
    back_right(1, right, rpre, g_in, wr, grad_right, scr)
    stores[3].start()
    sum_pump(1, 3)
    left_out(1)
    for kappa in range(2):

        @pl.when(core == kappa)
        def _():
            arrived(7 + kappa, dlbuf)

    scr[0:1024, :] = dlbuf[...].reshape(1024, 128).astype(F32)
    back_left(left, lpre, g_in, w_left[...], grad_left, scr)
    stores[2].start()

    all_drain(0, ls)
    all_drain(1, rs)
    all_drain(6, drsend)
    for kappa in range(2):
        part_drain(2 + kappa, kappa, tsend.at[kappa])
        part_drain(7 + kappa, kappa, dlsend.at[kappa])

        @pl.when(core == kappa)
        def _():
            all_drain(4 + kappa, dsend)

        for f in range(4):
            for s in range(FLOWS[f][2]):
                gather_copy(kappa, f, s).wait_send()
                sum_copy(kappa, f, s).wait_send()
    for store in stores:
        store.wait()


def hand_over_kernel(*refs):
    count = len(refs) // 2
    sems = refs[-1]
    copies = [pltpu.make_async_copy(refs[n], refs[count + n], sems.at[n]) for n in range(count)]
    for copy in copies:
        copy.start()
    for copy in copies:
        copy.wait()


VMEM_LIMIT = 56 * 1024 * 1024


def per_device(
    pair_out, pair_left, pair_right, ln_gain, ln_bias, w_left, w_right, w_gate, w_out,
    out_gain, out_bias, cotangent,
):
    vm = pl.BlockSpec(memory_space=pltpu.VMEM)
    hbm = pl.BlockSpec(memory_space=pl.ANY)
    gain, bias = ln_gain.reshape(1, 128), ln_bias.reshape(1, 128)
    o_gain, o_bias = out_gain.reshape(1, 128), out_bias.reshape(1, 128)

    def vmem(*shape, dtype=BF16):
        return pltpu.VMEM(shape, dtype)

    def wide(*shape):
        return pltpu.VMEM(shape, F32)

    pair, lefts = (32, 48, 128), (32, 32, 128)
    slots, half_slots = vmem(PLANE, 64, 128), vmem(PLANE, 32, 128)
    dma = pltpu.SemaphoreType.DMA
    outs = tuple(jax.ShapeDtypeStruct(shape, BF16) for shape in (pair, pair, lefts, pair))
    made = pl.pallas_call(
        triangle_kernel,
        out_shape=outs,
        in_specs=[hbm] * 4 + [vm] * 8,
        out_specs=(hbm,) * 4,
        scratch_shapes=[
            vmem(*lefts), vmem(*pair), vmem(*pair), vmem(*pair),
            vmem(*pair), vmem(*pair), vmem(*lefts), vmem(*pair),
            half_slots, slots,
            wide(8, 256, 128), wide(16, 256, 128),
            wide(1536, 128), wide(1536, 128), wide(1536, 128),
            vmem(NZ, PLANE, 32, 128), slots,
            vmem(2, HALF, 64, 128), slots,
            slots, slots,
            slots, slots,
            vmem(NZ, PLANE, 32, 128), vmem(2, 4, 4, QUART, 32, 128),
            vmem(2, HALF, 32, 128), half_slots,
            vmem(HS, 512, 512), vmem(HS, 512, 128),
            vmem(HS, 128, 512), vmem(HS, 512, 128),
            wide(2048, 128), wide(2048, 128), wide(HS, 512, 256),
            dma((4,)), dma((4,)), dma((9,)), dma((9,)),
            dma((2, 4, 4)), dma((2, 4, 4)), dma((2, 4, 4)), dma((2, 4, 4)),
        ],
        compiler_params=pltpu.CompilerParams(
            vmem_limit_bytes=VMEM_LIMIT, collective_id=0, has_side_effects=True
        ),
        name="triangle",
    )(
        pair_left, pair_right, pair_out, cotangent, gain, bias, w_left, w_right, w_gate, w_out,
        o_gain, o_bias,
    )
    return pl.pallas_call(
        hand_over_kernel,
        out_shape=outs,
        in_specs=[hbm] * 4,
        out_specs=(hbm,) * 4,
        scratch_shapes=[dma((4,))],
        compiler_params=pltpu.CompilerParams(vmem_limit_bytes=VMEM_LIMIT),
        name="hand_over",
    )(*made)


def solution(mesh):
    pairs, lefts = P("row", "col", None), P("col", "row", None)
    return jax.shard_map(
        per_device,
        mesh=mesh,
        in_specs=(pairs, lefts, pairs, P(), P(), P(), P(), P(), P(), P(), P(), pairs),
        out_specs=(pairs, pairs, lefts, pairs),
        check_vma=False,
    )
```

time: 411 us -> 148 us (0.36)
  waiting for transfers between devices: 263 us -> 0 us
  Pallas kernels: 0 us -> 147 us
  local copies, waits for them, and re-layouts: 74.8 us -> 0 us
  matrix products: 41.3 us -> 0 us
  other arithmetic: 16.9 us -> 0 us
  between operations: 14.2 us -> 0.8 us
    pallas_call x0 -> x2, Pallas kernels: none -> 147 us  [the longest x1 102 us: per_device(): pl.pallas_call(triangle_kernel, out_shape=outs, in_specs=[hbm] * 4 + [vm]...]
    reduce_scatter x2 -> x0, waiting for transfers between devices: 144 us -> none  [the longest x1 104 us: per_device(): lax.psum_scatter(jnp.einsum('ijh,kih->kjh', d_triangle, left_full, prefer...]
    all_gather x2 -> x0, waiting for transfers between devices: 118 us -> none  [the longest x1 62.2 us: per_device(): left_full = lax.all_gather(left_gated, 'col', axis=0, tiled=True)]
    all_gather x2 -> x0, local copies, waits for them, and re-layouts: 46.1 us -> none  [the longest x1 23.1 us: per_device(): right_full = lax.all_gather(right_gated, 'row', axis=0, tiled=True)]
    dot_general x11 -> x0, matrix products: 41.3 us -> none  [the longest x1 13.3 us: per_device(): jnp.einsum('kih,kjh->ijh', left_full, right_full, preferred_element_type=...]
    dot_general x2 -> x0, local copies, waits for them, and re-layouts: 18.9 us -> none  [the longest x1 9.8 us: per_device(): jnp.einsum('ijh,kih->kjh', d_triangle, left_full, preferred_element_type=...]
    convert_element_type x7 -> x0, other arithmetic: 8.69 us -> none  [the longest x2 2.97 us: project_back(): norm_back(d_normed.reshape(standard.shape), standard, inverse, gain)]
    unnamed x46 -> x0, local copies, waits for them, and re-layouts: 5.71 us -> none
  transfers between devices with their start and end apart: 4 -> 0, of which waited for: 4 -> 0; matrix products, arithmetic and copies ran while one was open for 15% -> 0% of each run, Pallas kernels for 0% -> 0%
where the time goes in v2:
time: 148 us
  Pallas kernels  147 us (99%)
    pallas_call x1, Pallas kernels, per_device(): pl.pallas_call(triangle_kernel, out_shape=outs, in_specs=[hbm] * 4 + [vm]...  102 us
    pallas_call x1, Pallas kernels, per_device(): pl.pallas_call(hand_over_kernel, out_shape=outs, in_specs=[hbm] * 4, out_...  44.8 us

profile of v2, /device:TPU:1, one launch (start us, length us, event | category | flops | bytes accessed | tf_op | source)
XLA Modules:
  0.0 148.0 jit_solution(10907190156363172943)
XLA Ops:
  0.6 102.4 %triangle.1 = (bf16[32,48,128]{2,1,0:T(8,128)(2,1)}, bf16[32,48,128]{2,1,0:T(8,128)(2,1)}, bf16[32,32,128]{2,1,0:T(8,128)(2,1)}, bf16[32,48,128]{2,1,0:T(8,128)(2,1)}) custom-call(bf16[32,32,128]{2,1,0:T(8,128)(2,1)} %left_hbm.1, bf16[32,48,128]{2,1,0:T(8,128)(2,1)} %right_hbm.1, bf16[32,48,128]{2,1,0:T(8,128)(2,1)} %out_hbm.1, ...), custom_call_target="tpu_custom_call" | custom-call | tf_op jit(solution)/shard_map/triangle/pallas_call | solution.py:575
  103.0 44.8 %hand_over.1 = (bf16[32,48,128]{2,1,0:T(8,128)(2,1)}, bf16[32,48,128]{2,1,0:T(8,128)(2,1)}, bf16[32,32,128]{2,1,0:T(8,128)(2,1)}, bf16[32,48,128]{2,1,0:T(8,128)(2,1)}) custom-call(bf16[32,48,128]{2,1,0:T(8,128)(2,1)} %get-tuple-element.8.refs_0_, bf16[32,48,128]{2,1,0:T(8,128)(2,1)} %get-tuple-element.9.refs_1_, ...), custom_call_target="tpu_custom_call" | custom-call | tf_op jit(solution)/shard_map/hand_over/pallas_call | solution.py:606

commit v3 on v2

--- a/solution.py
+++ b/solution.py
@@ -171,8 +171,14 @@
             gr[16 * b + n * 8 + t] = out[o : o + 48]
 
 
-FLOWS = ((1, 0, 4), (1, 1, 3), (-1, 0, 3), (-1, 1, 4))
-QUART = HALF // 2
+FLOWS = tuple(
+    (direction, part, 4 if (part < 2) == (direction > 0) else 3)
+    for part in range(4)
+    for direction in (1, -1)
+)
+NF = len(FLOWS)
+CHIPS = tuple((dx, dy, dl) for dx in (2, 1, 3, 0) for dy in (1, 0) for dl in (1, 0))
+QUART = HALF // 4
 
 
 def triangle_kernel(
@@ -192,21 +198,27 @@
     me16 = (row // 2) * 2 + yl
     me = core * HALF + me16
 
-    def plane_id(p):
-        q = lax.rem(p, HALF)
-        return {"row": (q // 2) * 2 + p // HALF, "col": lax.rem(q, 2) * NZ + z}
+    zs = [z] + [lax.rem(z + k, NZ) for k in range(1, NZ)]
+    x0, yh0 = row // 4, lax.rem(row // 2, 2)
+    xs = [x0] + [lax.rem(x0 + k, 4) for k in range(1, 4)]
+    yhs, yls, cores = (yh0, 1 - yh0), (yl, 1 - yl), (core, 1 - core)
+
+    def slot_of(dx, dy, dl):
+        return xs[dx] * 4 + yhs[dy] * 2 + yls[dl]
+
+    def plane_id(dx, dy, dl, core_there):
+        return {"row": xs[dx] * 4 + yhs[dy] * 2 + core_there, "col": yls[dl] * NZ + z}
 
     def z_id(direction):
-        return {"row": row, "col": yl * NZ + lax.rem(z + NZ + direction, NZ)}
+        return {"row": row, "col": yl * NZ + zs[direction % NZ]}
 
     barrier = pltpu.get_barrier_semaphore()
 
-    def greet(s, _):
-        p = lax.rem(me + s, PLANE)
-        pl.semaphore_signal(barrier, inc=1, device_id=plane_id(p), device_id_type=MESH)
-        return 0
-
-    lax.fori_loop(1, PLANE, greet, 0)
+    for dx, dy, dl in CHIPS:
+        for dc in range(2):
+            if (dx, dy, dl, dc) != (0, 0, 0, 0):
+                there = plane_id(dx, dy, dl, cores[dc])
+                pl.semaphore_signal(barrier, inc=1, device_id=there, device_id_type=MESH)
     for direction in (1, -1):
         pl.semaphore_signal(barrier, inc=1, device_id=z_id(direction), device_id_type=MESH)
 
@@ -230,26 +242,21 @@
     for load in loads:
         load.start()
 
-    def remote(n, src, dst, p):
+    def remote(n, src, dst, there):
         return pltpu.make_async_remote_copy(
-            src_ref=src, dst_ref=dst.at[me],
+            src_ref=src, dst_ref=dst,
             send_sem=a2a_send.at[n], recv_sem=a2a_recv.at[n],
-            device_id=plane_id(p), device_id_type=MESH,
+            device_id=there, device_id_type=MESH,
         )
 
     def all_start(n, src, dst, slot):
         pltpu.make_async_copy(src.at[me], dst.at[slot], a2a_recv.at[n]).start()
 
-        def send(s, _):
-            p = lax.rem(me + s, PLANE)
-            pltpu.make_async_remote_copy(
-                src_ref=src.at[p], dst_ref=dst.at[slot],
-                send_sem=a2a_send.at[n], recv_sem=a2a_recv.at[n],
-                device_id=plane_id(p), device_id_type=MESH,
-            ).start()
-            return 0
-
-        lax.fori_loop(1, PLANE, send, 0)
+        for dx, dy, dl in CHIPS:
+            for dc in range(2):
+                if (dx, dy, dl, dc) != (0, 0, 0, 0):
+                    p = cores[dc] * HALF + slot_of(dx, dy, dl)
+                    remote(n, src.at[p], dst.at[slot], plane_id(dx, dy, dl, cores[dc])).start()
 
     def all_drain(n, src):
         part = src.at[pl.ds(0, PLANE - 1)]
@@ -262,14 +269,12 @@
 
         @pl.when(core != kappa)
         def _():
-            remote(n, src.at[me16], dst, kappa * HALF + me16).start()
-
-        def send(s, _):
-            d = lax.rem(me16 + s, HALF)
-            remote(n, src.at[d], dst, kappa * HALF + d).start()
-            return 0
-
-        lax.fori_loop(1, HALF, send, 0)
+            remote(n, src.at[me16], dst.at[me], plane_id(0, 0, 0, kappa)).start()
+
+        for dx, dy, dl in CHIPS:
+            if (dx, dy, dl) != (0, 0, 0):
+                there = plane_id(dx, dy, dl, kappa)
+                remote(n, src.at[slot_of(dx, dy, dl)], dst.at[me], there).start()
 
     def part_drain(n, kappa, src):
         @pl.when(core == kappa)
@@ -284,12 +289,12 @@
     def arrived(n, dst):
         pltpu.make_async_copy(dst, dst, a2a_recv.at[n]).wait()
 
-    def z_slots(kappa, half):
-        return pl.ds(HALF * kappa + QUART * half, QUART)
+    def z_slots(kappa, part):
+        return pl.ds(HALF * kappa + QUART * part, QUART)
 
     def gather_copy(kappa, f, s):
-        direction, half, _ = FLOWS[f]
-        block = lbuf.at[lax.rem(z + NZ - direction * s, NZ), z_slots(kappa, half)]
+        direction, part, _ = FLOWS[f]
+        block = lbuf.at[zs[-direction * s % NZ], z_slots(kappa, part)]
         return pltpu.make_async_remote_copy(
             src_ref=block, dst_ref=block,
             send_sem=ag_send.at[kappa, f, s], recv_sem=ag_recv.at[kappa, f, s],
@@ -297,70 +302,61 @@
         )
 
     def gather_start(kappa):
-        for f in range(4):
+        for f in range(NF):
             gather_copy(kappa, f, 0).start()
 
     def gather_pump(kappa, s):
-        for f in range(4):
+        for f in range(NF):
             if s < FLOWS[f][2]:
                 gather_copy(kappa, f, s).wait_recv()
                 if s + 1 < FLOWS[f][2]:
                     gather_copy(kappa, f, s + 1).start()
 
     def unmix_left(kappa, zz):
-        def step(n, _):
-            ylk, q = n // 2, lax.rem(n, 2)
+        for n in range(4):
+            ylk, q = n // 2, n % 2
             x = [lbuf[zz, HALF * kappa + (4 * q + t) * 2 + ylk].astype(F32) for t in range(4)]
             y = exchange4(x)
             k0 = pl.multiple_of((ylk * NZ + zz) * 32, 32)
-            lanes = pl.ds(pl.multiple_of(256 * kappa + q * 128, 128), 128)
+            lanes = pl.ds(256 * kappa + q * 128, 128)
             for h in range(HS):
                 block = cat([y[b][8 * h : 8 * h + 8] for b in range(4)])
                 lm[h, pl.ds(k0, 32), lanes] = block.astype(BF16)
-            return 0
-
-        lax.fori_loop(0, 4, step, 0, unroll=2)
 
     def unmix_gathered(kappa, s):
         if s < 3:
-            unmix_left(kappa, lax.rem(z + NZ - s - 1, NZ))
-            unmix_left(kappa, lax.rem(z + s + 1, NZ))
+            unmix_left(kappa, zs[NZ - s - 1])
+            unmix_left(kappa, zs[s + 1])
         else:
-            unmix_left(kappa, lax.rem(z + 4, NZ))
+            unmix_left(kappa, zs[4])
 
     def unmix_pair(src, first, count, put):
-        def step(m, _):
+        for m in range(count):
             y = swap64(src[first + 2 * m].astype(F32), src[first + 2 * m + 1].astype(F32))
             for h in range(HS):
                 put(h, m, cat([y[g][16 * h : 16 * h + 16] for g in range(2)]).astype(BF16))
-            return 0
-
-        lax.fori_loop(0, count, step, 0, unroll=2)
 
     def unmix_right():
         for kappa in range(2):
 
             def put(h, m, block):
-                rm[h, pl.ds(pl.multiple_of((2 * m + kappa) * 32, 32), 32), :] = block
+                rm[h, pl.ds((2 * m + kappa) * 32, 32), :] = block
 
             unmix_pair(rbuf, HALF * kappa, 8, put)
 
     def unmix_d(kappa):
         def put(h, m, block):
-            dm[h, pl.ds(pl.multiple_of(256 * kappa + m * 32, 32), 32), :] = block
+            dm[h, pl.ds(256 * kappa + m * 32, 32), :] = block
 
         unmix_pair(dbuf, HALF * kappa, 8, put)
 
     def mix_pair(per_channel, blocks, put):
-        def step(m, _):
+        for m in range(blocks):
             for h in range(HS):
-                r0 = pl.multiple_of(h * per_channel + m * 32, 32)
+                r0 = h * per_channel + m * 32
                 y = swap64(scr[pl.ds(r0, 16), :], scr[pl.ds(r0 + 16, 16), :])
                 for v in range(2):
                     put(m, v, h, y[v].astype(BF16))
-            return 0
-
-        lax.fori_loop(0, blocks, step, 0, unroll=2)
 
     def triangle(kappa):
         for h in range(HS):
@@ -391,8 +387,8 @@
                 stores[1].start()
 
     def sum_copy(kappa, f, s):
-        direction, half, steps = FLOWS[f]
-        block = dls.at[lax.rem(z + NZ + direction * (steps - s), NZ), z_slots(kappa, half)]
+        direction, part, steps = FLOWS[f]
+        block = dls.at[zs[direction * (steps - s) % NZ], z_slots(kappa, part)]
         return pltpu.make_async_remote_copy(
             src_ref=block, dst_ref=rsbuf.at[kappa, f, s],
             send_sem=rs_send.at[kappa, f, s], recv_sem=rs_recv.at[kappa, f, s],
@@ -419,26 +415,26 @@
             return 0
 
         lax.fori_loop(0, 16, pack, 0, unroll=2)
-        for f in range(4):
+        for f in range(NF):
             sum_copy(kappa, f, 0).start()
 
     def sum_pump(kappa, s):
-        for f in range(4):
-            direction, half, steps = FLOWS[f]
+        for f in range(NF):
+            direction, part, steps = FLOWS[f]
             if s < steps:
                 sum_copy(kappa, f, s).wait_recv()
                 if s + 1 < steps:
-                    here = (lax.rem(z + NZ + direction * (steps - s - 1), NZ), z_slots(kappa, half))
+                    here = (zs[direction * (steps - s - 1) % NZ], z_slots(kappa, part))
                     dls[here] = (dls[here].astype(F32) + rsbuf[kappa, f, s].astype(F32)).astype(BF16)
                     sum_copy(kappa, f, s + 1).start()
 
     def left_out(kappa):
-        for half in range(2):
-            total = dls[z, z_slots(kappa, half)].astype(F32)
-            for f in range(4):
-                if FLOWS[f][1] == half:
+        for part in range(4):
+            total = dls[z, z_slots(kappa, part)].astype(F32)
+            for f in range(NF):
+                if FLOWS[f][1] == part:
                     total = total + rsbuf[kappa, f, FLOWS[f][2] - 1].astype(F32)
-            dlsend[kappa, QUART * half : QUART * half + QUART] = total.astype(BF16)
+            dlsend[kappa, QUART * part : QUART * part + QUART] = total.astype(BF16)
         part_start(7 + kappa, kappa, dlsend.at[kappa], dlbuf)
 
     loads[0].wait()
@@ -447,48 +443,49 @@
     all_start(0, ls, lbuf.at[z], me)
     loads[1].wait()
     project_right(right, g_in, b_in, w_right[...], rs, rpre, scr2)
-    all_start(1, rs, rbuf, me)
     arrived(0, lbuf.at[z])
     gather_start(0)
+    all_start(1, rs, rbuf, me)
     loads[2].wait()
-    gate_rows(pair_out, g_in, b_in, wg, gate_s, std_s, inv_s)
     unmix_left(0, z)
     unmix_left(1, z)
     gather_pump(0, 0)
+    gather_start(1)
+    gate_rows(pair_out, g_in, b_in, wg, gate_s, std_s, inv_s)
     unmix_gathered(0, 0)
+    gather_pump(0, 1)
+    gather_pump(1, 0)
+    unmix_gathered(0, 1)
+    unmix_gathered(1, 0)
+    gather_pump(0, 2)
+    gather_pump(1, 1)
     arrived(1, rbuf)
-    gather_pump(0, 1)
     unmix_right()
     for h in range(HS):
         rmt[h] = rm[h].T
-    unmix_gathered(0, 1)
-    gather_pump(0, 2)
-    gather_start(1)
     unmix_gathered(0, 2)
     gather_pump(0, 3)
     unmix_gathered(0, 3)
     loads[3].wait()
 
     triangle(0)
-    gather_pump(1, 0)
-    unmix_gathered(1, 0)
-    gather_pump(1, 1)
+    gather_pump(1, 2)
     unmix_gathered(1, 1)
-    slab(0, 0)
-    gather_pump(1, 2)
     unmix_gathered(1, 2)
-    slab(0, 1)
     gather_pump(1, 3)
     unmix_gathered(1, 3)
     triangle(1)
 
+    slab(0, 0)
+    slab(0, 1)
+    slab(1, 0)
+    slab(1, 1)
     left_sums(0)
-    slab(1, 0)
     sum_pump(0, 0)
-    slab(1, 1)
     sum_pump(0, 1)
+    left_sums(1)
     sum_pump(0, 2)
-    left_sums(1)
+    sum_pump(1, 0)
     sum_pump(0, 3)
     left_out(0)
 
@@ -496,21 +493,20 @@
         scr[512 * h : 512 * h + 512, :] = dot_nn(lm[h], dm[h])
 
     def put_right(m, v, h, block):
-        drsend[lax.rem(m, 2) * HALF + (m // 2) * 2 + v, 16 * h : 16 * h + 16, :] = block
+        drsend[(m % 2) * HALF + (m // 2) * 2 + v, 16 * h : 16 * h + 16, :] = block
 
     mix_pair(512, 16, put_right)
+    sum_pump(1, 1)
     all_start(6, drsend, drbuf, me)
-    sum_pump(1, 0)
-    sum_pump(1, 1)
+    sum_pump(1, 2)
+    sum_pump(1, 3)
+    left_out(1)
     arrived(6, drbuf)
     scr[...] = drbuf[...].reshape(2048, 128).astype(F32)
     wr = w_right[...]
     back_right(0, right, rpre, g_in, wr, grad_right, scr)
-    sum_pump(1, 2)
     back_right(1, right, rpre, g_in, wr, grad_right, scr)
     stores[3].start()
-    sum_pump(1, 3)
-    left_out(1)
     for kappa in range(2):
 
         @pl.when(core == kappa)
@@ -532,7 +528,7 @@
         def _():
             all_drain(4 + kappa, dsend)
 
-        for f in range(4):
+        for f in range(NF):
             for s in range(FLOWS[f][2]):
                 gather_copy(kappa, f, s).wait_send()
                 sum_copy(kappa, f, s).wait_send()
@@ -541,12 +537,16 @@
 
 
 def hand_over_kernel(*refs):
-    count = len(refs) // 2
-    sems = refs[-1]
-    copies = [pltpu.make_async_copy(refs[n], refs[count + n], sems.at[n]) for n in range(count)]
-    for copy in copies:
+    srcs, dsts, held = refs[:4], refs[4:8], refs[8:12]
+    in_sem, out_sem = refs[12:]
+    ins = [pltpu.make_async_copy(srcs[n], held[n], in_sem.at[n]) for n in range(4)]
+    outs = [pltpu.make_async_copy(held[n], dsts[n], out_sem.at[n]) for n in range(4)]
+    for copy in ins:
         copy.start()
-    for copy in copies:
+    for n in range(4):
+        ins[n].wait()
+        outs[n].start()
+    for copy in outs:
         copy.wait()
 
 
@@ -587,13 +587,13 @@
             vmem(2, HALF, 64, 128), slots,
             slots, slots,
             slots, slots,
-            vmem(NZ, PLANE, 32, 128), vmem(2, 4, 4, QUART, 32, 128),
+            vmem(NZ, PLANE, 32, 128), vmem(2, NF, 4, QUART, 32, 128),
             vmem(2, HALF, 32, 128), half_slots,
             vmem(HS, 512, 512), vmem(HS, 512, 128),
             vmem(HS, 128, 512), vmem(HS, 512, 128),
             wide(2048, 128), wide(2048, 128), wide(HS, 512, 256),
             dma((4,)), dma((4,)), dma((9,)), dma((9,)),
-            dma((2, 4, 4)), dma((2, 4, 4)), dma((2, 4, 4)), dma((2, 4, 4)),
+            dma((2, NF, 4)), dma((2, NF, 4)), dma((2, NF, 4)), dma((2, NF, 4)),
         ],
         compiler_params=pltpu.CompilerParams(
             vmem_limit_bytes=VMEM_LIMIT, collective_id=0, has_side_effects=True
@@ -608,7 +608,7 @@
         out_shape=outs,
         in_specs=[hbm] * 4,
         out_specs=(hbm,) * 4,
-        scratch_shapes=[dma((4,))],
+        scratch_shapes=[vmem(*pair), vmem(*pair), vmem(*lefts), vmem(*pair), dma((4,)), dma((4,))],
         compiler_params=pltpu.CompilerParams(vmem_limit_bytes=VMEM_LIMIT),
         name="hand_over",
     )(*made)

time: 148 us -> 92.4 us (0.62)
  Pallas kernels: 147 us -> 91.4 us
    pallas_call x1, Pallas kernels: 44.8 us -> 2.16 us  [per_device(): pl.pallas_call(hand_over_kernel, out_shape=outs, in_specs=[hbm] * 4, out_...]
    pallas_call x1, Pallas kernels: 102 us -> 89.3 us  [per_device(): pl.pallas_call(triangle_kernel, out_shape=outs, in_specs=[hbm] * 4 + [vm]...]
where the time goes in v3:
time: 92.4 us; the launch traced here: 92.2 us
  Pallas kernels  91.4 us (99%)
    pallas_call x1, Pallas kernels, per_device(): pl.pallas_call(triangle_kernel, out_shape=outs, in_specs=[hbm] * 4 + [vm]...  89.3 us
    pallas_call x1, Pallas kernels, per_device(): pl.pallas_call(hand_over_kernel, out_shape=outs, in_specs=[hbm] * 4, out_...  2.16 us

profile of v3, /device:TPU:1, one launch (start us, length us, event | category | flops | bytes accessed | tf_op | source)
XLA Modules:
  0.0 92.2 jit_solution(10679005206960614001)
XLA Ops:
  0.6 89.3 %triangle.1 = (bf16[32,48,128]{2,1,0:T(8,128)(2,1)}, bf16[32,48,128]{2,1,0:T(8,128)(2,1)}, bf16[32,32,128]{2,1,0:T(8,128)(2,1)}, bf16[32,48,128]{2,1,0:T(8,128)(2,1)}) custom-call(bf16[32,32,128]{2,1,0:T(8,128)(2,1)} %left_hbm.1, bf16[32,48,128]{2,1,0:T(8,128)(2,1)} %right_hbm.1, bf16[32,48,128]{2,1,0:T(8,128)(2,1)} %out_hbm.1, ...), custom_call_target="tpu_custom_call" | custom-call | tf_op jit(solution)/shard_map/triangle/pallas_call | solution.py:575
  89.9 2.2 %hand_over.1 = (bf16[32,48,128]{2,1,0:T(8,128)(2,1)}, bf16[32,48,128]{2,1,0:T(8,128)(2,1)}, bf16[32,32,128]{2,1,0:T(8,128)(2,1)}, bf16[32,48,128]{2,1,0:T(8,128)(2,1)}) custom-call(bf16[32,48,128]{2,1,0:T(8,128)(2,1)} %get-tuple-element.8.refs_0_, bf16[32,48,128]{2,1,0:T(8,128)(2,1)} %get-tuple-element.9.refs_1_, ...), custom_call_target="tpu_custom_call" | custom-call | tf_op jit(solution)/shard_map/hand_over/pallas_call | solution.py:606

commit v4 on v3

--- a/solution.py
+++ b/solution.py
@@ -66,18 +66,24 @@
     return z0, z1, z2, z3
 
 
-def project_left(left, g, bi, w, ls, lpre, scr):
+def gate_of(pre):
+    squash = jax.nn.sigmoid(pre[128:])
+    gated = squash * pre[:128]
+    return gated, cat([squash, gated * (1.0 - squash)])
+
+
+def project_left(left, g, bi, w, ls, lfac, scr):
     x = cat([left[8 * b + a] for a in range(8) for b in range(4)]).astype(F32)
     standard, _ = standardize(x)
     pre = dot_nt(w.T, (standard * g + bi).astype(BF16))
-    gated = jax.nn.sigmoid(pre[128:]) * pre[:128]
+    gated, factors = gate_of(pre)
     for a in range(8):
-        lpre[a] = pre[:, 128 * a : 128 * a + 128]
+        lfac[a] = factors[:, 128 * a : 128 * a + 128]
         scr[pl.ds(a, 128, stride=8), :] = gated[:, 128 * a : 128 * a + 128]
     ls[...] = scr[0:1024, :].astype(BF16).reshape(PLANE, 32, 128)
 
 
-def project_right(right, g, bi, w, rs, rpre, scr):
+def project_right(right, g, bi, w, rs, rfac, scr):
     zeros = jnp.zeros((16, 128), F32)
     wr = w.T
 
@@ -87,9 +93,9 @@
         normed = standard * g + bi
         normed = cat([y for t in range(16) for y in (normed[48 * t : 48 * t + 48], zeros)])
         pre = dot_nt(wr, normed.astype(BF16))
-        gated = jax.nn.sigmoid(pre[128:]) * pre[:128]
+        gated, factors = gate_of(pre)
         for t in range(8):
-            rpre[n * 8 + t] = pre[:, 128 * t : 128 * t + 128]
+            rfac[n * 8 + t] = factors[:, 128 * t : 128 * t + 128]
             scr[pl.ds(n * 8 + t, 128, stride=16), :] = gated[:, 128 * t : 128 * t + 128]
         return 0
 
@@ -97,12 +103,16 @@
     rs[...] = scr[...].astype(BF16).reshape(PLANE, 64, 128)
 
 
-def gate_rows(pair_out, g, bi, wg, gate_s, std_s, inv_s):
+def gate_rows(pair_out, cot, g, bi, wg, wo, g_tri, gate_s, std_s, inv_s, up_s):
     def step(n, _):
         x = cat([pair_out[16 * b + n * 8 + t] for t in range(8) for b in range(2)]).astype(F32)
         standard, inverse = standardize(x)
         rows = pl.ds(pl.multiple_of(n * 768, 768), 768)
-        gate_s[rows, :] = jax.nn.sigmoid(dot_nn((standard * g + bi).astype(BF16), wg))
+        gate = jax.nn.sigmoid(dot_nn((standard * g + bi).astype(BF16), wg))
+        up = cat([cot[16 * b + n * 8 + t] for t in range(8) for b in range(2)]).astype(F32)
+        scaled = dot_nt((up * gate).astype(BF16), wo) * g_tri
+        up_s[rows, :] = scaled - jnp.mean(scaled, axis=-1, keepdims=True)
+        gate_s[rows, :] = gate
         std_s[rows, :] = standard
         inv_s[rows, :] = jnp.broadcast_to(inverse, standard.shape)
         return 0
@@ -110,57 +120,68 @@
     lax.fori_loop(0, 2, step, 0)
 
 
-def slab_rows(n, scr, scr2, cot, g_in, g_tri, b_tri, wg, wo, gate_s, std_s, inv_s, result, grad_out):
+def slab_back(n, scr, scr2, up_s, tri_s):
     zeros = jnp.zeros((16, 128), F32)
     parts = []
     for t in range(8):
         tri = scr[pl.ds(n * 8 + t, 128, stride=16), :].T
         parts += [tri[0:48], tri[64:112]]
-    tri = cat(parts)
-    up = cat([cot[16 * b + n * 8 + t] for t in range(8) for b in range(2)]).astype(F32)
+    tri_std, tri_inv = standardize(cat(parts))
     rows = pl.ds(n * 768, 768)
-    gate, out_std, out_inv = gate_s[rows, :], std_s[rows, :], inv_s[rows, :]
-    tri_std, tri_inv = standardize(tri)
-    proj = dot_nn((tri_std * g_tri + b_tri).astype(BF16), wo)
-    gated_up = up * gate
-    d_tri = norm_back(dot_nt(gated_up.astype(BF16), wo), tri_std, tri_inv, g_tri)
-    res = (gate * proj).astype(BF16)
-    d_gate = (gated_up * proj * (1.0 - gate)).astype(BF16)
-    g_out = norm_back(dot_nt(d_gate, wg), out_std, out_inv, g_in).astype(BF16)
+    tri_s[rows, :] = tri_std
+    up = up_s[rows, :]
+    d_tri = tri_inv * (up - tri_std * jnp.mean(up * tri_std, axis=-1, keepdims=True))
     for t in range(8):
-        for b in range(2):
-            o = (2 * t + b) * 48
-            result[16 * b + n * 8 + t] = res[o : o + 48]
-            grad_out[16 * b + n * 8 + t] = g_out[o : o + 48]
         o = 96 * t
         padded = cat([d_tri[o : o + 48], zeros, d_tri[o + 48 : o + 96], zeros])
         scr2[pl.ds(n * 8 + t, 128, stride=16), :] = padded.T
 
 
-def d_pre_of(d, pre):
-    p, q = pre[:128], pre[128:]
-    squash = jax.nn.sigmoid(q)
-    d_p = d * squash
-    return cat([d_p, d_p * p * (1.0 - squash)]).astype(BF16)
-
-
-def back_left(left, lpre, g, w, gl, scr):
-    d = cat([scr[pl.ds(a, 128, stride=8), :] for a in range(8)], axis=1)
-    pre = cat([lpre[a] for a in range(8)], axis=1)
-    e = dot_nn(w, d_pre_of(d, pre)).T
+def slab_rows(cot, g_in, g_tri, b_tri, wg, wo, gate_s, std_s, inv_s, tri_s, result, grad_out):
+    def step(n, _):
+        rows = pl.ds(pl.multiple_of(n * 768, 768), 768)
+        up = cat([cot[16 * b + n * 8 + t] for t in range(8) for b in range(2)]).astype(F32)
+        gate = gate_s[rows, :]
+        proj = dot_nn((tri_s[rows, :] * g_tri + b_tri).astype(BF16), wo)
+        res = (gate * proj).astype(BF16)
+        d_gate = (up * gate * proj * (1.0 - gate)).astype(BF16)
+        g_out = norm_back(dot_nt(d_gate, wg), std_s[rows, :], inv_s[rows, :], g_in).astype(BF16)
+        for t in range(8):
+            for b in range(2):
+                o = (2 * t + b) * 48
+                result[16 * b + n * 8 + t] = res[o : o + 48]
+                grad_out[16 * b + n * 8 + t] = g_out[o : o + 48]
+        return 0
+
+    lax.fori_loop(0, 2, step, 0)
+
+
+def d_pre_of(d, factors):
+    return cat([d * factors[:128], d * factors[128:]]).astype(BF16)
+
+
+def prepare_left(left, lstd, linv):
     x = cat([left[8 * b + a] for a in range(8) for b in range(4)]).astype(F32)
     standard, inverse = standardize(x)
-    out = norm_back(e, standard, inverse, g).astype(BF16)
+    lstd[...] = standard
+    linv[...] = jnp.broadcast_to(inverse, standard.shape)
+
+
+def back_left(lstd, linv, lfac, g, w, gl, scr):
+    d = cat([scr[pl.ds(a, 128, stride=8), :] for a in range(8)], axis=1)
+    factors = cat([lfac[a] for a in range(8)], axis=1)
+    e = dot_nn(w, d_pre_of(d, factors)).T
+    out = norm_back(e, lstd[...], linv[...], g).astype(BF16)
     for a in range(8):
         for b in range(4):
             o = 128 * a + 32 * b
             gl[8 * b + a] = out[o : o + 32]
 
 
-def back_right(n, right, rpre, g, w, gr, scr):
+def back_right(n, right, rfac, g, w, gr, scr):
     d = cat([scr[pl.ds(n * 8 + t, 128, stride=16), :] for t in range(8)], axis=1)
-    pre = cat([rpre[n * 8 + t] for t in range(8)], axis=1)
-    e = dot_nn(w, d_pre_of(d, pre)).T
+    factors = cat([rfac[n * 8 + t] for t in range(8)], axis=1)
+    e = dot_nn(w, d_pre_of(d, factors)).T
     e = cat([y for t in range(8) for y in (e[128 * t : 128 * t + 48], e[128 * t + 64 : 128 * t + 112])])
     x = cat([right[16 * b + n * 8 + t] for t in range(8) for b in range(2)]).astype(F32)
     standard, inverse = standardize(x)
@@ -185,7 +206,7 @@
     left_hbm, right_hbm, out_hbm, cot_hbm, gain, bias, w_left, w_right, w_gate, w_out, o_gain, o_bias,
     result_hbm, grad_out_hbm, grad_left_hbm, grad_right_hbm,
     left, right, pair_out, cot, result, grad_out, grad_left, grad_right,
-    ls, rs, lpre, rpre, gate_s, std_s, inv_s,
+    ls, rs, lfac, rfac, gate_s, std_s, inv_s, up_s, tri_s, lstd, linv,
     lbuf, rbuf, tsend, tbuf, dsend, dbuf, drsend, drbuf, dls, rsbuf, dlsend, dlbuf,
     lm, rm, rmt, dm, scr, scr2, big,
     in_sem, out_sem, a2a_send, a2a_recv, ag_send, ag_recv, rs_send, rs_recv,
@@ -377,14 +398,10 @@
             if n == 0:
                 arrived(2 + kappa, tbuf)
                 scr[...] = tbuf[...].reshape(2048, 128).astype(F32)
-            slab_rows(
-                n, scr, scr2, cot, g_in, g_tri, b_tri, wg, wo, gate_s, std_s, inv_s, result, grad_out
-            )
+            slab_back(n, scr, scr2, up_s, tri_s)
             if n == 1:
                 dsend[...] = scr2[...].astype(BF16).reshape(PLANE, 64, 128)
                 all_start(4 + kappa, dsend, dbuf, me)
-                stores[0].start()
-                stores[1].start()
 
     def sum_copy(kappa, f, s):
         direction, part, steps = FLOWS[f]
@@ -401,22 +418,24 @@
         for h in range(HS):
             big[h] = dot_nt(rm[h], dm[h, 256 * kappa : 256 * kappa + 256, :])
 
-        def pack(c, _):
-            k0 = pl.multiple_of(c * 32, 32)
-            for q in range(2):
-                x = [
-                    cat([big[h, pl.ds(k0 + 8 * b, 8), 128 * q : 128 * q + 128] for h in range(HS)])
-                    for b in range(4)
-                ]
-                y = exchange4(x)
-                for t in range(4):
-                    slot = HALF * kappa + (4 * q + t) * 2 + c // NZ
-                    dls[lax.rem(c, NZ), slot] = y[t].astype(BF16)
-            return 0
-
-        lax.fori_loop(0, 16, pack, 0, unroll=2)
+        def pack(zz):
+            for ylk in range(2):
+                k0 = pl.multiple_of((ylk * NZ + zz) * 32, 32)
+                for q in range(2):
+                    x = [
+                        cat([big[h, pl.ds(k0 + 8 * b, 8), 128 * q : 128 * q + 128] for h in range(HS)])
+                        for b in range(4)
+                    ]
+                    y = exchange4(x)
+                    for t in range(4):
+                        dls[zz, HALF * kappa + (4 * q + t) * 2 + ylk] = y[t].astype(BF16)
+
+        for k in (4, 3, 5):
+            pack(zs[k])
         for f in range(NF):
             sum_copy(kappa, f, 0).start()
+        for k in (2, 6, 1, 7, 0):
+            pack(zs[k])
 
     def sum_pump(kappa, s):
         for f in range(NF):
@@ -438,20 +457,21 @@
         part_start(7 + kappa, kappa, dlsend.at[kappa], dlbuf)
 
     loads[0].wait()
-    project_left(left, g_in, b_in, w_left[...], ls, lpre, scr)
+    project_left(left, g_in, b_in, w_left[...], ls, lfac, scr)
     pl.semaphore_wait(barrier, PLANE - 1 + 2)
     all_start(0, ls, lbuf.at[z], me)
     loads[1].wait()
-    project_right(right, g_in, b_in, w_right[...], rs, rpre, scr2)
+    project_right(right, g_in, b_in, w_right[...], rs, rfac, scr2)
+    loads[2].wait()
+    loads[3].wait()
+    gate_rows(pair_out, cot, g_in, b_in, wg, wo, g_tri, gate_s, std_s, inv_s, up_s)
     arrived(0, lbuf.at[z])
     gather_start(0)
     all_start(1, rs, rbuf, me)
-    loads[2].wait()
     unmix_left(0, z)
     unmix_left(1, z)
     gather_pump(0, 0)
     gather_start(1)
-    gate_rows(pair_out, g_in, b_in, wg, gate_s, std_s, inv_s)
     unmix_gathered(0, 0)
     gather_pump(0, 1)
     gather_pump(1, 0)
@@ -466,7 +486,6 @@
     unmix_gathered(0, 2)
     gather_pump(0, 3)
     unmix_gathered(0, 3)
-    loads[3].wait()
 
     triangle(0)
     gather_pump(1, 2)
@@ -480,32 +499,35 @@
     slab(0, 1)
     slab(1, 0)
     slab(1, 1)
+    slab_rows(cot, g_in, g_tri, b_tri, wg, wo, gate_s, std_s, inv_s, tri_s, result, grad_out)
+    stores[0].start()
+    stores[1].start()
     left_sums(0)
+    left_sums(1)
     sum_pump(0, 0)
+    sum_pump(1, 0)
+    for h in range(HS):
+        scr[512 * h : 512 * h + 512, :] = dot_nn(lm[h], dm[h])
+
+    def put_right(m, v, h, block):
+        drsend[(m % 2) * HALF + (m // 2) * 2 + v, 16 * h : 16 * h + 16, :] = block
+
+    mix_pair(512, 16, put_right)
+    all_start(6, drsend, drbuf, me)
     sum_pump(0, 1)
-    left_sums(1)
+    sum_pump(1, 1)
+    prepare_left(left, lstd, linv)
     sum_pump(0, 2)
-    sum_pump(1, 0)
+    sum_pump(1, 2)
     sum_pump(0, 3)
     left_out(0)
-
-    for h in range(HS):
-        scr[512 * h : 512 * h + 512, :] = dot_nn(lm[h], dm[h])
-
-    def put_right(m, v, h, block):
-        drsend[(m % 2) * HALF + (m // 2) * 2 + v, 16 * h : 16 * h + 16, :] = block
-
-    mix_pair(512, 16, put_right)
-    sum_pump(1, 1)
-    all_start(6, drsend, drbuf, me)
-    sum_pump(1, 2)
     sum_pump(1, 3)
     left_out(1)
     arrived(6, drbuf)
     scr[...] = drbuf[...].reshape(2048, 128).astype(F32)
     wr = w_right[...]
-    back_right(0, right, rpre, g_in, wr, grad_right, scr)
-    back_right(1, right, rpre, g_in, wr, grad_right, scr)
+    back_right(0, right, rfac, g_in, wr, grad_right, scr)
+    back_right(1, right, rfac, g_in, wr, grad_right, scr)
     stores[3].start()
     for kappa in range(2):
 
@@ -514,7 +536,7 @@
             arrived(7 + kappa, dlbuf)
 
     scr[0:1024, :] = dlbuf[...].reshape(1024, 128).astype(F32)
-    back_left(left, lpre, g_in, w_left[...], grad_left, scr)
+    back_left(lstd, linv, lfac, g_in, w_left[...], grad_left, scr)
     stores[2].start()
 
     all_drain(0, ls)
@@ -583,6 +605,7 @@
             half_slots, slots,
             wide(8, 256, 128), wide(16, 256, 128),
             wide(1536, 128), wide(1536, 128), wide(1536, 128),
+            wide(1536, 128), wide(1536, 128), wide(1024, 128), wide(1024, 128),
             vmem(NZ, PLANE, 32, 128), slots,
             vmem(2, HALF, 64, 128), slots,
             slots, slots,

time: 92.4 us -> 87.5 us (0.947)
  Pallas kernels: 91.4 us -> 86.5 us
    pallas_call x1, Pallas kernels: 89.3 us -> 84.4 us  [per_device(): pl.pallas_call(triangle_kernel, out_shape=outs, in_specs=[hbm] * 4 + [vm]...]
where the time goes in v4:
time: 87.5 us; the launch traced here: 87.3 us
  Pallas kernels  86.5 us (99%)
    pallas_call x1, Pallas kernels, per_device(): pl.pallas_call(triangle_kernel, out_shape=outs, in_specs=[hbm] * 4 + [vm]...  84.4 us
    pallas_call x1, Pallas kernels, per_device(): pl.pallas_call(hand_over_kernel, out_shape=outs, in_specs=[hbm] * 4, out_...  2.16 us

profile of v4, /device:TPU:1, one launch (start us, length us, event | category | flops | bytes accessed | tf_op | source)
XLA Modules:
  0.0 87.3 jit_solution(5618344698544876183)
XLA Ops:
  0.6 84.4 %triangle.1 = (bf16[32,48,128]{2,1,0:T(8,128)(2,1)}, bf16[32,48,128]{2,1,0:T(8,128)(2,1)}, bf16[32,32,128]{2,1,0:T(8,128)(2,1)}, bf16[32,48,128]{2,1,0:T(8,128)(2,1)}) custom-call(bf16[32,32,128]{2,1,0:T(8,128)(2,1)} %left_hbm.1, bf16[32,48,128]{2,1,0:T(8,128)(2,1)} %right_hbm.1, bf16[32,48,128]{2,1,0:T(8,128)(2,1)} %out_hbm.1, ...), custom_call_target="tpu_custom_call" | custom-call | tf_op jit(solution)/shard_map/triangle/pallas_call | solution.py:597
  85.0 2.2 %hand_over.1 = (bf16[32,48,128]{2,1,0:T(8,128)(2,1)}, bf16[32,48,128]{2,1,0:T(8,128)(2,1)}, bf16[32,32,128]{2,1,0:T(8,128)(2,1)}, bf16[32,48,128]{2,1,0:T(8,128)(2,1)}) custom-call(bf16[32,48,128]{2,1,0:T(8,128)(2,1)} %get-tuple-element.8.refs_0_, bf16[32,48,128]{2,1,0:T(8,128)(2,1)} %get-tuple-element.9.refs_1_, ...), custom_call_target="tpu_custom_call" | custom-call | tf_op jit(solution)/shard_map/hand_over/pallas_call | solution.py:629

commit v5 on v4

--- a/solution.py
+++ b/solution.py
@@ -203,14 +203,18 @@
 
 
 def triangle_kernel(
-    left_hbm, right_hbm, out_hbm, cot_hbm, gain, bias, w_left, w_right, w_gate, w_out, o_gain, o_bias,
-    result_hbm, grad_out_hbm, grad_left_hbm, grad_right_hbm,
-    left, right, pair_out, cot, result, grad_out, grad_left, grad_right,
-    ls, rs, lfac, rfac, gate_s, std_s, inv_s, up_s, tri_s, lstd, linv,
-    lbuf, rbuf, tsend, tbuf, dsend, dbuf, drsend, drbuf, dls, rsbuf, dlsend, dlbuf,
-    lm, rm, rmt, dm, scr, scr2, big,
-    in_sem, out_sem, a2a_send, a2a_recv, ag_send, ag_recv, rs_send, rs_recv,
+    left_hbm, right_hbm, out_hbm, cot_hbm, *rest
 ):
+    small_hbm, outs_hbm, small, rest = rest[:8], rest[8:12], rest[12:20], rest[20:]
+    result_hbm, grad_out_hbm, grad_left_hbm, grad_right_hbm = outs_hbm
+    gain, bias, w_left, w_right, w_gate, w_out, o_gain, o_bias = small
+    (
+        left, right, pair_out, cot, result, grad_out, grad_left, grad_right,
+        ls, rs, lfac, rfac, gate_s, std_s, inv_s, up_s, tri_s, lstd, linv,
+        lbuf, rbuf, tsend, tbuf, dsend, dbuf, drsend, drbuf, dls, rsbuf, dlsend, dlbuf,
+        lm, rm, rmt, dm, scr, scr2, big,
+        small_sem, in_sem, out_sem, a2a_send, a2a_recv, ag_send, ag_recv, rs_send, rs_recv,
+    ) = rest
     row = lax.axis_index("row")
     col = lax.axis_index("col")
     z = lax.rem(col, NZ)
@@ -260,7 +264,13 @@
             )
         )
     ]
-    for load in loads:
+    small_loads = [
+        pltpu.make_async_copy(small_hbm[n], small[n], small_sem.at[n]) for n in range(8)
+    ]
+    loads[0].start()
+    for load in small_loads:
+        load.start()
+    for load in loads[1:]:
         load.start()
 
     def remote(n, src, dst, there):
@@ -389,6 +399,8 @@
         mix_pair(256, 8, put)
         part_start(2 + kappa, kappa, tsend.at[kappa], tbuf)
 
+    for load in small_loads:
+        load.wait()
     g_in, b_in, g_tri, b_tri = gain[...], bias[...], o_gain[...], o_bias[...]
     wg, wo = w_gate[...], w_out[...]
 
@@ -432,8 +444,10 @@
 
         for k in (4, 3, 5):
             pack(zs[k])
-        for f in range(NF):
-            sum_copy(kappa, f, 0).start()
+            for f in range(NF):
+                direction, _, steps = FLOWS[f]
+                if direction * steps % NZ == k:
+                    sum_copy(kappa, f, 0).start()
         for k in (2, 6, 1, 7, 0):
             pack(zs[k])
 
@@ -499,9 +513,6 @@
     slab(0, 1)
     slab(1, 0)
     slab(1, 1)
-    slab_rows(cot, g_in, g_tri, b_tri, wg, wo, gate_s, std_s, inv_s, tri_s, result, grad_out)
-    stores[0].start()
-    stores[1].start()
     left_sums(0)
     left_sums(1)
     sum_pump(0, 0)
@@ -516,6 +527,9 @@
     all_start(6, drsend, drbuf, me)
     sum_pump(0, 1)
     sum_pump(1, 1)
+    slab_rows(cot, g_in, g_tri, b_tri, wg, wo, gate_s, std_s, inv_s, tri_s, result, grad_out)
+    stores[0].start()
+    stores[1].start()
     prepare_left(left, lstd, linv)
     sum_pump(0, 2)
     sum_pump(1, 2)
@@ -561,15 +575,19 @@
 def hand_over_kernel(*refs):
     srcs, dsts, held = refs[:4], refs[4:8], refs[8:12]
     in_sem, out_sem = refs[12:]
-    ins = [pltpu.make_async_copy(srcs[n], held[n], in_sem.at[n]) for n in range(4)]
-    outs = [pltpu.make_async_copy(held[n], dsts[n], out_sem.at[n]) for n in range(4)]
-    for copy in ins:
-        copy.start()
-    for n in range(4):
-        ins[n].wait()
-        outs[n].start()
-    for copy in outs:
-        copy.wait()
+    pieces = [(n, p) for p in range(2) for n in range(4)]
+
+    def copy(froms, tos, sems, n, p):
+        rows = pl.ds(16 * p, 16)
+        return pltpu.make_async_copy(froms[n].at[rows], tos[n].at[rows], sems.at[n, p])
+
+    for n, p in pieces:
+        copy(srcs, held, in_sem, n, p).start()
+    for n, p in pieces:
+        copy(srcs, held, in_sem, n, p).wait()
+        copy(held, dsts, out_sem, n, p).start()
+    for n, p in pieces:
+        copy(held, dsts, out_sem, n, p).wait()
 
 
 VMEM_LIMIT = 56 * 1024 * 1024
@@ -579,7 +597,6 @@
     pair_out, pair_left, pair_right, ln_gain, ln_bias, w_left, w_right, w_gate, w_out,
     out_gain, out_bias, cotangent,
 ):
-    vm = pl.BlockSpec(memory_space=pltpu.VMEM)
     hbm = pl.BlockSpec(memory_space=pl.ANY)
     gain, bias = ln_gain.reshape(1, 128), ln_bias.reshape(1, 128)
     o_gain, o_bias = out_gain.reshape(1, 128), out_bias.reshape(1, 128)
@@ -591,15 +608,17 @@
         return pltpu.VMEM(shape, F32)
 
     pair, lefts = (32, 48, 128), (32, 32, 128)
+    small = [wide(1, 128), wide(1, 128), vmem(128, 256), vmem(128, 256)]
+    small += [vmem(128, 128), vmem(128, 128), wide(1, 128), wide(1, 128)]
     slots, half_slots = vmem(PLANE, 64, 128), vmem(PLANE, 32, 128)
     dma = pltpu.SemaphoreType.DMA
     outs = tuple(jax.ShapeDtypeStruct(shape, BF16) for shape in (pair, pair, lefts, pair))
     made = pl.pallas_call(
         triangle_kernel,
         out_shape=outs,
-        in_specs=[hbm] * 4 + [vm] * 8,
+        in_specs=[hbm] * 12,
         out_specs=(hbm,) * 4,
-        scratch_shapes=[
+        scratch_shapes=small + [
             vmem(*lefts), vmem(*pair), vmem(*pair), vmem(*pair),
             vmem(*pair), vmem(*pair), vmem(*lefts), vmem(*pair),
             half_slots, slots,
@@ -615,7 +634,7 @@
             vmem(HS, 512, 512), vmem(HS, 512, 128),
             vmem(HS, 128, 512), vmem(HS, 512, 128),
             wide(2048, 128), wide(2048, 128), wide(HS, 512, 256),
-            dma((4,)), dma((4,)), dma((9,)), dma((9,)),
+            dma((8,)), dma((4,)), dma((4,)), dma((9,)), dma((9,)),
             dma((2, NF, 4)), dma((2, NF, 4)), dma((2, NF, 4)), dma((2, NF, 4)),
         ],
         compiler_params=pltpu.CompilerParams(
@@ -631,7 +650,7 @@
         out_shape=outs,
         in_specs=[hbm] * 4,
         out_specs=(hbm,) * 4,
-        scratch_shapes=[vmem(*pair), vmem(*pair), vmem(*lefts), vmem(*pair), dma((4,)), dma((4,))],
+        scratch_shapes=[vmem(*pair), vmem(*pair), vmem(*lefts), vmem(*pair), dma((4, 2)), dma((4, 2))],
         compiler_params=pltpu.CompilerParams(vmem_limit_bytes=VMEM_LIMIT),
         name="hand_over",
     )(*made)

time: 87.5 us -> 86.6 us (0.990)
    pallas_call x1, Pallas kernels: 84.4 us -> 83.5 us  [per_device(): pl.pallas_call(triangle_kernel, out_shape=outs, in_specs=[hbm] * 12, out_...]
where the time goes in v5:
time: 86.6 us; the launch traced here: 86.5 us
  Pallas kernels  85.7 us (99%)
    pallas_call x1, Pallas kernels, per_device(): pl.pallas_call(triangle_kernel, out_shape=outs, in_specs=[hbm] * 12, out_...  83.5 us
    pallas_call x1, Pallas kernels, per_device(): pl.pallas_call(hand_over_kernel, out_shape=outs, in_specs=[hbm] * 4, out_...  2.24 us

profile of v5, /device:TPU:1, one launch (start us, length us, event | category | flops | bytes accessed | tf_op | source)
XLA Modules:
  0.0 86.5 jit_solution(7998272727280615693)
XLA Ops:
  0.6 83.5 %triangle.1 = (bf16[32,48,128]{2,1,0:T(8,128)(2,1)}, bf16[32,48,128]{2,1,0:T(8,128)(2,1)}, bf16[32,32,128]{2,1,0:T(8,128)(2,1)}, bf16[32,48,128]{2,1,0:T(8,128)(2,1)}) custom-call(bf16[32,32,128]{2,1,0:T(8,128)(2,1)} %left_hbm.1, bf16[32,48,128]{2,1,0:T(8,128)(2,1)} %right_hbm.1, bf16[32,48,128]{2,1,0:T(8,128)(2,1)} %out_hbm.1, ...), custom_call_target="tpu_custom_call" | custom-call | tf_op jit(solution)/shard_map/triangle/pallas_call | solution.py:616
  84.1 2.2 %hand_over.1 = (bf16[32,48,128]{2,1,0:T(8,128)(2,1)}, bf16[32,48,128]{2,1,0:T(8,128)(2,1)}, bf16[32,32,128]{2,1,0:T(8,128)(2,1)}, bf16[32,48,128]{2,1,0:T(8,128)(2,1)}) custom-call(bf16[32,48,128]{2,1,0:T(8,128)(2,1)} %get-tuple-element.8.refs_0_, bf16[32,48,128]{2,1,0:T(8,128)(2,1)} %get-tuple-element.9.refs_1_, ...), custom_call_target="tpu_custom_call" | custom-call | tf_op jit(solution)/shard_map/hand_over/pallas_call | solution.py:648

commit v6 on v5

--- a/solution.py
+++ b/solution.py
@@ -473,19 +473,28 @@
     loads[0].wait()
     project_left(left, g_in, b_in, w_left[...], ls, lfac, scr)
     pl.semaphore_wait(barrier, PLANE - 1 + 2)
-    all_start(0, ls, lbuf.at[z], me)
+    @pl.when(core == 0)
+    def _():
+        all_start(0, ls, lbuf.at[z], me)
+
     loads[1].wait()
     project_right(right, g_in, b_in, w_right[...], rs, rfac, scr2)
+
+    @pl.when(core == 1)
+    def _():
+        all_start(9, ls, lbuf.at[z], me)
+
     loads[2].wait()
     loads[3].wait()
     gate_rows(pair_out, cot, g_in, b_in, wg, wo, g_tri, gate_s, std_s, inv_s, up_s)
-    arrived(0, lbuf.at[z])
+    arrived(0, lbuf.at[z, pl.ds(0, HALF)])
     gather_start(0)
+    unmix_left(0, z)
+    gather_pump(0, 0)
+    arrived(9, lbuf.at[z, pl.ds(HALF, HALF)])
+    gather_start(1)
     all_start(1, rs, rbuf, me)
-    unmix_left(0, z)
     unmix_left(1, z)
-    gather_pump(0, 0)
-    gather_start(1)
     unmix_gathered(0, 0)
     gather_pump(0, 1)
     gather_pump(1, 0)
@@ -553,7 +562,12 @@
     back_left(lstd, linv, lfac, g_in, w_left[...], grad_left, scr)
     stores[2].start()
 
-    all_drain(0, ls)
+    for kappa in range(2):
+
+        @pl.when(core == kappa)
+        def _():
+            all_drain(9 * kappa, ls)
+
     all_drain(1, rs)
     all_drain(6, drsend)
     for kappa in range(2):
@@ -634,7 +648,7 @@
             vmem(HS, 512, 512), vmem(HS, 512, 128),
             vmem(HS, 128, 512), vmem(HS, 512, 128),
             wide(2048, 128), wide(2048, 128), wide(HS, 512, 256),
-            dma((8,)), dma((4,)), dma((4,)), dma((9,)), dma((9,)),
+            dma((8,)), dma((4,)), dma((4,)), dma((10,)), dma((10,)),
             dma((2, NF, 4)), dma((2, NF, 4)), dma((2, NF, 4)), dma((2, NF, 4)),
         ],
         compiler_params=pltpu.CompilerParams(

time: 86.6 us -> 86.4 us (level)
  no operation moved by 1% of the time
where the time goes in v6:
time: 86.4 us; the launch traced here: 86.3 us
  Pallas kernels  85.5 us (99%)
    pallas_call x1, Pallas kernels, per_device(): pl.pallas_call(triangle_kernel, out_shape=outs, in_specs=[hbm] * 12, out_...  83.3 us
    pallas_call x1, Pallas kernels, per_device(): pl.pallas_call(hand_over_kernel, out_shape=outs, in_specs=[hbm] * 4, out_...  2.24 us

profile of v6, /device:TPU:1, one launch (start us, length us, event | category | flops | bytes accessed | tf_op | source)
XLA Modules:
  0.0 86.3 jit_solution(15858872887964586990)
XLA Ops:
  0.6 83.3 %triangle.1 = (bf16[32,48,128]{2,1,0:T(8,128)(2,1)}, bf16[32,48,128]{2,1,0:T(8,128)(2,1)}, bf16[32,32,128]{2,1,0:T(8,128)(2,1)}, bf16[32,48,128]{2,1,0:T(8,128)(2,1)}) custom-call(bf16[32,32,128]{2,1,0:T(8,128)(2,1)} %left_hbm.1, bf16[32,48,128]{2,1,0:T(8,128)(2,1)} %right_hbm.1, bf16[32,48,128]{2,1,0:T(8,128)(2,1)} %out_hbm.1, ...), custom_call_target="tpu_custom_call" | custom-call | tf_op jit(solution)/shard_map/triangle/pallas_call | solution.py:630
  83.9 2.2 %hand_over.1 = (bf16[32,48,128]{2,1,0:T(8,128)(2,1)}, bf16[32,48,128]{2,1,0:T(8,128)(2,1)}, bf16[32,32,128]{2,1,0:T(8,128)(2,1)}, bf16[32,48,128]{2,1,0:T(8,128)(2,1)}) custom-call(bf16[32,48,128]{2,1,0:T(8,128)(2,1)} %get-tuple-element.8.refs_0_, bf16[32,48,128]{2,1,0:T(8,128)(2,1)} %get-tuple-element.9.refs_1_, ...), custom_call_target="tpu_custom_call" | custom-call | tf_op jit(solution)/shard_map/hand_over/pallas_call | solution.py:662
